TPU v7x, 32 devices: a whole 2x2x4 slice. The times are simulated.
32 devices in a mesh: seq: 16 (over z, y, x), batch: 2 (over core).
Axes of the slice: x: 2, y: 2, z: 4, core: 2. Of those that a mesh axis runs over, the one named last changes fastest.
Arguments:
- block_input: float32 [2, 4096, 768], P('batch', 'seq'), may hold values from -6 to 6
- ln1_gain: float32 [768], replicated, may hold values from 0.5 to 1.5
- ln1_bias: float32 [768], replicated, may hold values from -0.5 to 0.5
- w_qkv: bfloat16 [768, 2304], replicated, may hold values from -0.3125 to 0.3125
- w_out: bfloat16 [768, 768], replicated, may hold values from -0.875 to 0.875
- ln2_gain: float32 [768], replicated, may hold values from 0.5 to 1.5
- ln2_bias: float32 [768], replicated, may hold values from -0.5 to 0.5
- w_up: bfloat16 [768, 3072], replicated, may hold values from -0.21875 to 0.21875
- w_down: bfloat16 [3072, 768], replicated, may hold values from -0.109375 to 0.109375
- length_draw: int32 [2], P('batch'), may hold values from 0 to 16383
- threshold_index: int32 [1], replicated, may hold values from 0 to 255
- grad_out: float32 [2, 4096, 768], P('batch', 'seq'), may hold values from -6 to 6
Outputs:
- layer_out: float32 [2, 4096, 768], P('batch', 'seq')
- grad_x: float32 [2, 4096, 768], P('batch', 'seq')
- grad_ln1_gain: float32 [768], replicated
- grad_ln1_bias: float32 [768], replicated
- grad_w_qkv: float32 [768, 2304], replicated
- grad_w_out: float32 [768, 768], replicated
- grad_ln2_gain: float32 [768], replicated
- grad_ln2_bias: float32 [768], replicated
- grad_w_up: float32 [768, 3072], replicated
- grad_w_down: float32 [3072, 768], replicated
- pruned_share: float32 [1], replicated
Inputs may be any that keep to these rules, and one draw needn't show every extreme that they name: Group g holds one sequence of 3841 + (length_draw[g] mod 256) tokens from its first slot; the other slots are padding. The threshold is threshold_index / 128.
All inputs are finite; a program needn't handle non-finite values.
Results may differ from a plain program's by a relative error of at most 0.012.
The roundings to bfloat16 on the way count: a program that leaves them out, or rounds other values in their place, can miss the bound.
Values may be sent and summed in bfloat16 or wider, within the bound.
A program may use at most 512 MiB of HBM per device.

v0:
```python
import functools

import jax
import jax.numpy as jnp
from jax import lax
from jax.experimental import pallas as pl
from jax.experimental.pallas import tpu as pltpu
from jax.sharding import PartitionSpec as P

HEADS = 12
HEAD_DIM = 64
TEAMS = 4
TEAM_HEADS = HEADS // TEAMS
TEAM_WIDTH = TEAM_HEADS * HEAD_DIM
QUERY_WIDTH = TEAM_WIDTH + HEAD_DIM

epsilon = 1e-05
negative = -1e30
select_scale = 3.0
VMEM_BYTES = 60 * 2**20
MESH = pl.DeviceIdType.MESH


def peers_of(scope):
    lanes = lax.axis_size("seq") // TEAMS
    me = lax.axis_index("seq")
    team, lane = me // lanes, lax.rem(me, lanes)
    if scope == "team":
        return lane, lanes, lambda k: {"seq": team * lanes + k}
    if scope == "lane":
        return team, TEAMS, lambda k: {"seq": k * lanes + lane}
    if scope == "core":
        return lax.axis_index("batch"), 2, lambda k: {"batch": k}
    return me, lanes * TEAMS, lambda k: {"seq": k}


def scope_size(scope):
    count = lax.axis_size("seq")
    return {"team": count // TEAMS, "lane": TEAMS, "core": 2, "all": count}[scope]


def greet(scopes):
    barrier = pltpu.get_barrier_semaphore()
    number = 0
    for scope in scopes:
        mine, peers, device_of = peers_of(scope)
        for k in range(1, peers):
            pl.semaphore_signal(
                barrier, inc=1, device_id=device_of(lax.rem(mine + k, peers)), device_id_type=MESH
            )
        number += peers - 1
    pl.semaphore_wait(barrier, number)


def push(source, destination, send, receive, target, start=True):
    copy = pltpu.make_async_remote_copy(
        src_ref=source,
        dst_ref=destination,
        send_sem=send,
        recv_sem=receive,
        device_id=target,
        device_id_type=MESH,
    )
    if start:
        copy.start()
    return copy


def part_of(kind, ref, k):
    if kind == "gather":
        return ref
    if kind == "spread":
        return ref.at[k]
    if kind == "second":
        return ref.at[:, k]
    half = ref.shape[1] // 2
    return ref.at[:, pl.ds(pl.multiple_of(k * half, 128), half)]


def remote_copies(plan, sources, targets, send, receive, start=True):
    copies = []
    for n, (scope, kind) in enumerate(plan):
        mine, peers, device_of = peers_of(scope)
        for k in range(1, peers):
            peer = lax.rem(mine + k, peers)
            copies.append(
                push(
                    part_of(kind, sources[n], peer),
                    targets[n].at[mine],
                    send.at[n, k],
                    receive.at[n, k],
                    device_of(peer),
                    start,
                )
            )
    return copies


def exchange_shapes(plan, arrays):
    shapes = []
    for (scope, kind), x in zip(plan, arrays):
        shape = x.shape
        if kind == "gather":
            shape = (scope_size(scope),) + shape
        if kind == "half":
            shape = (2, shape[0], shape[1] // 2)
        if kind == "second":
            shape = (shape[1], shape[0]) + shape[2:]
        shapes.append(jax.ShapeDtypeStruct(shape, x.dtype))
    return shapes


def exchange_sems(plan):
    number, most = len(plan), max(scope_size(scope) for scope, _ in plan)
    return [
        pltpu.SemaphoreType.DMA((number, most)),
        pltpu.SemaphoreType.DMA((number, most)),
        pltpu.SemaphoreType.DMA((number,)),
    ]


def scopes_of(plan):
    return [x for x in ("core", "team", "lane", "all") if x in [scope for scope, _ in plan]]


def exchange(plan, arrays, collective):
    number = len(arrays)
    shapes = exchange_shapes(plan, arrays)

    def body(*refs):
        sources, targets = refs[:number], refs[number : 2 * number]
        send, receive, local = refs[2 * number : 2 * number + 3]
        through = refs[2 * number + 3 :]
        greet(scopes_of(plan))
        copies = remote_copies(plan, sources, targets, send, receive)
        inward = []
        for n, (scope, kind) in enumerate(plan):
            mine = peers_of(scope)[0]
            copy = pltpu.make_async_copy(part_of(kind, sources[n], mine), through[n], local.at[n])
            copy.start()
            inward.append(copy)
        for n, (scope, kind) in enumerate(plan):
            mine = peers_of(scope)[0]
            inward[n].wait()
            copy = pltpu.make_async_copy(through[n], targets[n].at[mine], local.at[n])
            copy.start()
            copies.append(copy)
        for copy in copies:
            copy.wait()

    return pl.pallas_call(
        body,
        out_shape=shapes,
        in_specs=[pl.BlockSpec(memory_space=pl.ANY)] * number,
        out_specs=[pl.BlockSpec(memory_space=pl.ANY)] * number,
        scratch_shapes=exchange_sems(plan) + [pltpu.VMEM(x.shape[1:], x.dtype) for x in shapes],
        compiler_params=pltpu.CompilerParams(
            collective_id=collective, has_side_effects=True, vmem_limit_bytes=VMEM_BYTES
        ),
    )(*arrays)


def dot(left, right):
    return jnp.dot(left, right, preferred_element_type=jnp.float32)


def project_body(
    tokens_ref,
    gain_ref,
    bias_ref,
    w_ref,
    lane_ref,
    weight_ref,
    query_ref,
    key_ref,
    value_ref,
    held,
    ready,
    windows,
    firsts,
    hop_send,
    hop_recv,
    team_send,
    team_recv,
    weight_sems,
    local_sems,
):
    lanes = lax.axis_size("seq") // TEAMS
    me = lax.axis_index("seq")
    team, lane = me // lanes, lax.rem(me, lanes)
    width = tokens_ref.shape[1]
    wide = windows.shape[2]
    start = (3 * team // 2) * 128
    loads = []
    for part in range(3):
        at = pl.ds(pl.multiple_of(part * width + start, 128), wide)
        loads.append(pltpu.make_async_copy(w_ref.at[:, at], windows.at[part], weight_sems.at[part]))
    for part in range(2):
        at = pl.ds(part * width, 128)
        loads.append(
            pltpu.make_async_copy(w_ref.at[:, at], firsts.at[part], weight_sems.at[3 + part])
        )
    for load in loads:
        load.start()
    tokens = tokens_ref[...]
    row_mean = jnp.mean(tokens, axis=1, keepdims=True)
    centred = tokens - row_mean
    variance = jnp.mean(centred * centred, axis=1, keepdims=True)
    normed = centred * lax.rsqrt(variance + epsilon) * gain_ref[...] + bias_ref[...]
    held[team] = normed.astype(jnp.bfloat16)
    greet(["team", "lane"])

    def hop(side, distance, start=True):
        block = team - distance if side == 0 else team + distance
        target = me + lanes if side == 0 else me - lanes
        return push(
            held.at[block],
            held.at[block],
            hop_send.at[side, distance],
            hop_recv.at[side, distance],
            {"seq": target},
            start,
        )

    @pl.when(team < TEAMS - 1)
    def _():
        hop(0, 0)

    @pl.when(team > 0)
    def _():
        hop(1, 0)

    for load in loads:
        load.wait()
    odd = lax.rem(team, 2) == 1
    pieces = []
    for part in range(3):
        window = windows[part]
        pieces.append(
            jnp.where(odd, window[:, wide - TEAM_WIDTH :], window[:, :TEAM_WIDTH])
        )
        if part < 2:
            pieces.append(firsts[part][:, :HEAD_DIM])
    weight_ref[...] = jnp.concatenate(pieces, axis=1)

    def block_copies(block, start):
        copies = []
        for k in range(1, lanes):
            target = {"seq": team * lanes + lax.rem(lane + k, lanes)}
            copies.append(
                push(
                    ready.at[block],
                    query_ref.at[lane, block],
                    team_send.at[block, k],
                    team_recv.at[block, k],
                    target,
                    start,
                )
            )
        for n, (source, destination) in enumerate(
            ((ready.at[block], query_ref.at[lane, block]), (held.at[block], lane_ref.at[block]))
        ):
            copy = pltpu.make_async_copy(source, destination, local_sems.at[n, block])
            if start:
                copy.start()
            copies.append(copy)
        return copies

    def project(block):
        result = dot(held[block], weight_ref[...]).astype(jnp.bfloat16)
        ready[block] = result[:, :QUERY_WIDTH] * jnp.bfloat16(HEAD_DIM ** (-0.5))
        block_copies(block, True)
        key_ref[block] = result[:, QUERY_WIDTH : 2 * QUERY_WIDTH]
        value_ref[block] = result[:, 2 * QUERY_WIDTH :]

    project(team)

    def arrive(step, _):
        distance, side = step // 2 + 1, lax.rem(step, 2)
        for which in range(2):
            block = team - distance if which == 0 else team + distance
            there = (block >= 0) if which == 0 else (block < TEAMS)
            further = (team < TEAMS - 1) if which == 0 else (team > 0)

            @pl.when((side == which) & there)
            def _():
                hop(which, distance - 1, False).wait_recv()

                @pl.when(further)
                def _():
                    hop(which, distance)

                project(block)

        return 0

    lax.fori_loop(0, 2 * (TEAMS - 1), arrive, 0)
    for distance in range(TEAMS - 1):

        @pl.when((team < TEAMS - 1) & (team >= distance))
        def _():
            hop(0, distance, False).wait_send()

        @pl.when((team > 0) & (team + distance < TEAMS))
        def _():
            hop(1, distance, False).wait_send()

    for block in range(TEAMS):
        for copy in block_copies(block, False):
            copy.wait()


def project(tokens, gain, bias, weight, collective):
    lanes = lax.axis_size("seq") // TEAMS
    rows, width = tokens.shape
    inside = pl.BlockSpec(memory_space=pltpu.VMEM)
    anywhere = pl.BlockSpec(memory_space=pl.ANY)
    columns = 2 * QUERY_WIDTH + TEAM_WIDTH
    low = jnp.bfloat16
    dma = pltpu.SemaphoreType.DMA
    return pl.pallas_call(
        project_body,
        out_shape=[
            jax.ShapeDtypeStruct((TEAMS, rows, width), low),
            jax.ShapeDtypeStruct((width, columns), low),
            jax.ShapeDtypeStruct((lanes, TEAMS, rows, QUERY_WIDTH), low),
            jax.ShapeDtypeStruct((TEAMS, rows, QUERY_WIDTH), low),
            jax.ShapeDtypeStruct((TEAMS, rows, TEAM_WIDTH), low),
        ],
        in_specs=[inside, inside, inside, anywhere],
        out_specs=[anywhere, inside, anywhere, inside, inside],
        scratch_shapes=[
            pltpu.VMEM((TEAMS, rows, width), low),
            pltpu.VMEM((TEAMS, rows, QUERY_WIDTH), low),
            pltpu.VMEM((3, width, 256), low),
            pltpu.VMEM((2, width, 128), low),
            dma((2, TEAMS)),
            dma((2, TEAMS)),
            dma((TEAMS, lanes)),
            dma((TEAMS, lanes)),
            dma((5,)),
            dma((2, TEAMS)),
        ],
        compiler_params=pltpu.CompilerParams(
            collective_id=collective, has_side_effects=True, vmem_limit_bytes=VMEM_BYTES
        ),
    )(tokens, gain[None], bias[None], weight)


def fold(tile):
    return jnp.sum(tile.reshape(tile.shape[0] // 8, 8, tile.shape[1]), axis=0)


def attend_body(
    length_ref,
    threshold_ref,
    q_ref,
    kk_ref,
    vv_ref,
    out_ref,
    mass_ref,
    carried_ref,
    excess_ref,
    key_heads,
    value_rows,
    running,
    logits,
    out_all,
    mass_all,
    lane_out,
    lane_mass,
    joined_out,
    joined_mass,
    home_out,
    home_mass,
    lane_send,
    lane_recv,
    home_send,
    home_recv,
    *,
    blocks,
    rows,
):
    lanes = blocks // TEAMS
    me = lax.axis_index("seq")
    team, lane = me // lanes, lax.rem(me, lanes)
    i = pl.program_id(0)
    scale = select_scale / (blocks * rows)
    key_iota = lax.broadcasted_iota(jnp.int32, (rows, rows), 0)
    query_iota = lax.broadcasted_iota(jnp.int32, (rows, rows), 1)

    def part_copies(j, start):
        z, owner = j // lanes, lax.rem(j, lanes)
        return [
            push(
                source.at[j],
                destination.at[z, lane],
                lane_send.at[n, j],
                lane_recv.at[n, z, lane],
                {"seq": team * lanes + owner},
                start,
            )
            for n, (source, destination) in enumerate(
                ((out_all, lane_out), (mass_all, lane_mass))
            )
        ]

    def home_copies(z, start):
        return [
            push(
                source.at[z],
                destination.at[team],
                home_send.at[n, z],
                home_recv.at[n, team],
                {"seq": z * lanes + lane},
                start,
            )
            for n, (source, destination) in enumerate(
                ((joined_out, home_out), (joined_mass, home_mass))
            )
        ]

    def join(z):
        for k in range(1, lanes):
            other = lax.rem(lane + k, lanes)
            for n, buffer in enumerate((lane_out, lane_mass)):
                pltpu.make_async_copy(
                    buffer.at[z, other], buffer.at[z, other], lane_recv.at[n, z, other]
                ).wait()
        masses = [lane_mass[z, p] for p in range(lanes)]
        peak = masses[0]
        for p in range(1, lanes):
            peak = jnp.maximum(peak, masses[p])
        shares = [jnp.exp(mass - peak) for mass in masses]
        whole = shares[0]
        for p in range(1, lanes):
            whole = whole + shares[p]
        joined_mass[z] = peak + jnp.log(whole)
        inverse = 1.0 / whole
        for h in range(TEAM_HEADS):
            span = slice(h * HEAD_DIM, (h + 1) * HEAD_DIM)
            mixed = None
            for p in range(lanes):
                share = (shares[p] * inverse)[h : h + 1, :]
                part = lane_out[z, p, span, :].astype(jnp.float32) * share
                mixed = part if p == 0 else mixed + part
            joined_out[z, span, :] = mixed.astype(jnp.bfloat16)

        @pl.when(team != z)
        def _():
            home_copies(z, True)

        @pl.when(team == z)
        def _():
            home_out[team] = joined_out[z]
            home_mass[team] = joined_mass[z]

    @pl.when(i == 0)
    def _():
        greet(["team", "lane"])
        running[...] = jnp.zeros_like(running)
        excess_ref[...] = jnp.zeros_like(excess_ref)
        for z in range(TEAMS):
            for h in range(TEAM_HEADS):
                key_heads[h, z] = kk_ref[z, :, h * HEAD_DIM : (h + 1) * HEAD_DIM]
            first = kk_ref[z, :, TEAM_WIDTH:]
            if z == 0:
                slot = lax.broadcasted_iota(jnp.int32, first.shape, 0) + lane * rows
                first = jnp.where(slot >= 1, first, jnp.zeros_like(first))
            key_heads[TEAM_HEADS, z] = first
            value_rows[z] = vv_ref[z].T

    active = jnp.where(i >= lane, (i - lane) // lanes + 1, 0)
    threshold = threshold_ref[0]

    @pl.when(active == 0)
    def _():
        out_all[i] = jnp.zeros((TEAM_WIDTH, rows), jnp.bfloat16)
        mass_all[i] = jnp.full((8, rows), negative, jnp.float32)

    def work(count):
        q_rows = q_ref[0, 0].T
        heads = [q_rows[h * HEAD_DIM : (h + 1) * HEAD_DIM] for h in range(TEAM_HEADS + 1)]
        earlier = jnp.where(key_iota < query_iota, scale, 0.0).astype(jnp.bfloat16)
        every = jnp.full((rows, rows), scale, jnp.bfloat16)
        last = ((count - 1) * lanes + lane) * rows + key_iota
        query_pos = i * rows + query_iota
        peaks = [None] * TEAM_HEADS
        for z in range(count):
            first = jnp.maximum(dot(key_heads[TEAM_HEADS, z], heads[TEAM_HEADS]), 0.0)
            if z == count - 1:
                first = jnp.where(last < query_pos, first, 0.0)
            first = first.astype(jnp.bfloat16)
            carried = running[z] + dot(first, earlier)
            running[z] = running[z] + dot(first, every)

            if z == count - 1:
                carried = jnp.where(last <= query_pos, carried, -negative)
            carried_ref[0, z] = carried
            for h in range(TEAM_HEADS):
                logit = dot(key_heads[h, z], heads[h]) - carried
                logits[h, z] = logit
                peak = jnp.max(logit.reshape(rows // 8, 8, rows), axis=0)
                peaks[h] = peak if z == 0 else jnp.maximum(peaks[h], peak)
        mass_all[i] = jnp.zeros((8, rows), jnp.float32)
        for h in range(TEAM_HEADS):
            peak = jnp.max(peaks[h], axis=0, keepdims=True)
            mass, mixed = None, None
            for z in range(count):
                terms = jnp.exp(logits[h, z] - peak)
                part = fold(terms)
                values = value_rows[z, h * HEAD_DIM : (h + 1) * HEAD_DIM, :]
                product = dot(values, terms.astype(jnp.bfloat16))
                mass = part if z == 0 else mass + part
                mixed = product if z == 0 else mixed + product
            mass = jnp.sum(mass, axis=0, keepdims=True)
            out_all[i, h * HEAD_DIM : (h + 1) * HEAD_DIM, :] = (mixed * (1.0 / mass)).astype(
                jnp.bfloat16
            )
            mass_all[i, h : h + 1, :] = peak + jnp.log(mass)

        @pl.when(lax.rem(i, TEAMS) == team)
        def _():
            total = None
            for z in range(count):
                carried = carried_ref[0, z]
                if z == count - 1:
                    carried = jnp.where(last < query_pos, carried, 0.0)
                part = fold(jnp.clip(carried - threshold, 0.0, 1.0))
                total = part if z == 0 else total + part
            valid = i * rows + lax.broadcasted_iota(jnp.int32, (8, rows), 1) < length_ref[0]
            excess_ref[...] += jnp.where(valid, total, 0.0)

    for count in range(1, TEAMS + 1):
        pl.when(active == count)(functools.partial(work, count))

    @pl.when(lax.rem(i, lanes) != lane)
    def _():
        part_copies(i, True)

    @pl.when(lax.rem(i, lanes) == lane)
    def _():
        lane_out[i // lanes, lane] = out_all[i]
        lane_mass[i // lanes, lane] = mass_all[i]

    for z in range(TEAMS - 1):
        pl.when(i == (z + 1) * lanes + 1)(functools.partial(join, z))

    @pl.when(i == blocks - 1)
    def _():
        join(TEAMS - 1)

        def drain(j, _):
            @pl.when(lax.rem(j, lanes) != lane)
            def _():
                for copy in part_copies(j, False):
                    copy.wait_send()

            return 0

        lax.fori_loop(0, blocks, drain, 0)
        for z in range(TEAMS):

            @pl.when(team != z)
            def _():
                for copy in home_copies(z, False):
                    copy.wait_send()
                for n, buffer in enumerate((home_out, home_mass)):
                    pltpu.make_async_copy(
                        buffer.at[z], buffer.at[z], home_recv.at[n, z]
                    ).wait()

        out_ref[...] = home_out[...]
        mass_ref[...] = home_mass[...]

def attend(length, threshold, queries, keys, values, blocks, rows, collective):
    lanes = blocks // TEAMS
    smem = pl.BlockSpec(memory_space=pltpu.SMEM)
    whole = pl.BlockSpec((TEAMS, rows, QUERY_WIDTH), lambda i: (0, 0, 0))
    return pl.pallas_call(
        functools.partial(attend_body, blocks=blocks, rows=rows),
        grid=(blocks,),
        in_specs=[
            smem,
            smem,
            pl.BlockSpec(
                (1, 1, rows, QUERY_WIDTH), lambda i: (lax.rem(i, lanes), i // lanes, 0, 0)
            ),
            whole,
            pl.BlockSpec((TEAMS, rows, TEAM_WIDTH), lambda i: (0, 0, 0)),
        ],
        out_specs=[
            pl.BlockSpec((TEAMS, TEAM_WIDTH, rows), lambda i: (0, 0, 0)),
            pl.BlockSpec((TEAMS, 8, rows), lambda i: (0, 0, 0)),
            pl.BlockSpec((1, TEAMS, rows, rows), lambda i: (i, 0, 0, 0)),
            pl.BlockSpec((8, rows), lambda i: (0, 0)),
        ],
        out_shape=[
            jax.ShapeDtypeStruct((TEAMS, TEAM_WIDTH, rows), jnp.bfloat16),
            jax.ShapeDtypeStruct((TEAMS, 8, rows), jnp.float32),
            jax.ShapeDtypeStruct((blocks, TEAMS, rows, rows), jnp.float32),
            jax.ShapeDtypeStruct((8, rows), jnp.float32),
        ],
        scratch_shapes=[
            pltpu.VMEM((TEAM_HEADS + 1, TEAMS, rows, HEAD_DIM), jnp.bfloat16),
            pltpu.VMEM((TEAMS, TEAM_WIDTH, rows), jnp.bfloat16),
            pltpu.VMEM((TEAMS, rows, rows), jnp.float32),
            pltpu.VMEM((TEAM_HEADS, TEAMS, rows, rows), jnp.float32),
            pltpu.VMEM((blocks, TEAM_WIDTH, rows), jnp.bfloat16),
            pltpu.VMEM((blocks, 8, rows), jnp.float32),
            pltpu.VMEM((TEAMS, lanes, TEAM_WIDTH, rows), jnp.bfloat16),
            pltpu.VMEM((TEAMS, lanes, 8, rows), jnp.float32),
            pltpu.VMEM((TEAMS, TEAM_WIDTH, rows), jnp.bfloat16),
            pltpu.VMEM((TEAMS, 8, rows), jnp.float32),
            pltpu.VMEM((TEAMS, TEAM_WIDTH, rows), jnp.bfloat16),
            pltpu.VMEM((TEAMS, 8, rows), jnp.float32),
            pltpu.SemaphoreType.DMA((2, blocks)),
            pltpu.SemaphoreType.DMA((2, TEAMS, lanes)),
            pltpu.SemaphoreType.DMA((2, TEAMS)),
            pltpu.SemaphoreType.DMA((2, TEAMS)),
        ],
        compiler_params=pltpu.CompilerParams(
            collective_id=collective, has_side_effects=True, vmem_limit_bytes=VMEM_BYTES
        ),
    )(length, threshold, queries, keys, values)


reduce_plan = [("lane", "second"), ("team", "spread"), ("team", "spread")]


def added(parts):
    total = parts[0].astype(jnp.float32)
    for part in parts[1:]:
        total = total + part.astype(jnp.float32)
    return total.astype(jnp.bfloat16)


def attend_back_body(
    q_ref,
    grad_ref,
    stat_ref,
    carried_ref,
    kk_ref,
    vv_ref,
    *refs,
    blocks,
    rows,
):
    plan = reduce_plan
    sources, refs = refs[:3], refs[3:]
    (query_grad_ref, key_grad_ref, value_grad_ref), reduced, refs = refs[:3], refs[3:6], refs[6:]
    key_heads, key_rows, value_heads, running, key_sum, value_sum = refs[:6]
    grad_all, stat_all, grad_send, grad_recv, send, receive, local = refs[6:13]
    targets = refs[13:]
    lanes = blocks // TEAMS
    me = lax.axis_index("seq")
    team, lane = me // lanes, lax.rem(me, lanes)
    step = pl.program_id(0)
    i = blocks - 1 - step
    scale = select_scale / (blocks * rows)
    span = [slice(h * HEAD_DIM, (h + 1) * HEAD_DIM) for h in range(TEAM_HEADS + 1)]
    key_iota = lax.broadcasted_iota(jnp.int32, (rows, rows), 0)
    query_iota = lax.broadcasted_iota(jnp.int32, (rows, rows), 1)

    place, owner = i // lanes, lax.rem(i, lanes)

    def grad_copies(z, start):
        return [
            push(
                buffer.at[lane, z],
                buffer.at[lane, z],
                grad_send.at[n, z, k],
                grad_recv.at[n, z, lane],
                {"seq": team * lanes + lax.rem(lane + k, lanes)},
                start,
            )
            for k in range(1, lanes)
            for n, buffer in enumerate((grad_all, stat_all))
        ]

    def own_copy(n):
        scope, kind = plan[n]
        mine = peers_of(scope)[0]
        return pltpu.make_async_copy(
            part_of(kind, sources[n], mine), targets[n].at[mine], local.at[n]
        )

    def plan_copies(scope, start):
        chosen = [n for n in range(len(plan)) if plan[n][0] == scope]
        copies = []
        for n in chosen:
            copies += remote_copies(
                plan[n : n + 1],
                sources[n : n + 1],
                targets[n : n + 1],
                send.at[n : n + 1],
                receive.at[n : n + 1],
                start,
            )
        return copies

    @pl.when(step == 0)
    def _():
        greet(["team", "lane"])
        grad_all[lane] = grad_ref[...]
        stat_all[lane] = stat_ref[...]
        for z in reversed(range(TEAMS)):
            grad_copies(z, True)
        plan_copies("lane", True)
        for n in range(len(plan)):
            own_copy(n).start()
        running[...] = jnp.zeros_like(running)
        key_sum[...] = jnp.zeros_like(key_sum)
        value_sum[...] = jnp.zeros_like(value_sum)
        for z in range(TEAMS):
            for h in range(TEAM_HEADS + 1):
                key_heads[h, z] = kk_ref[z, :, span[h]]
            for h in range(TEAM_HEADS):
                value_heads[h, z] = vv_ref[z, :, span[h]]
            key_rows[z] = kk_ref[z].T
        first = kk_ref[0, :, span[TEAM_HEADS]]
        slot = lax.broadcasted_iota(jnp.int32, first.shape, 0) + lane * rows
        key_heads[TEAM_HEADS, 0] = jnp.where(slot >= 1, first, jnp.zeros_like(first))

    @pl.when(step == 2)
    def _():
        plan_copies("team", True)

    @pl.when(owner != lane)
    def _():
        for n, buffer in enumerate((grad_all, stat_all)):
            at = buffer.at[owner, place]
            pltpu.make_async_copy(at, at, grad_recv.at[n, place, owner]).wait()

    active = jnp.where(i >= lane, (i - lane) // lanes + 1, 0)

    @pl.when(active == 0)
    def _():
        query_grad_ref[...] = jnp.zeros_like(query_grad_ref)

    def work(count):
        q_rows = q_ref[0, 0].T
        grad_rows = grad_all[owner, place].T
        q_row = [q_rows[span[h]] for h in range(TEAM_HEADS + 1)]
        q_col = [q_ref[0, 0, :, span[h]] for h in range(TEAM_HEADS + 1)]
        grad_row = [grad_rows[span[h]] for h in range(TEAM_HEADS)]
        grad_col = [grad_all[owner, place, :, span[h]] for h in range(TEAM_HEADS)]
        mass = [stat_all[owner, place, h : h + 1, :] for h in range(TEAM_HEADS)]
        inner = [stat_all[owner, place, TEAM_HEADS + h : TEAM_HEADS + h + 1, :] for h in range(TEAM_HEADS)]
        later = jnp.where(key_iota > query_iota, -scale, 0.0).astype(jnp.bfloat16)
        every = jnp.full((rows, rows), -scale, jnp.bfloat16)
        last = ((count - 1) * lanes + lane) * rows + key_iota
        query_pos = i * rows + query_iota
        sums = [None] * (TEAM_HEADS + 1)
        for z in range(count):
            carried = carried_ref[0, z]
            total = None
            for h in range(TEAM_HEADS):
                probs = jnp.exp(dot(key_heads[h, z], q_row[h]) - carried - mass[h])
                value_sum[h, z] += dot(probs.astype(jnp.bfloat16), grad_col[h])
                grad_logit = probs * (dot(value_heads[h, z], grad_row[h]) - inner[h])
                total = grad_logit if h == 0 else total + grad_logit
                low = grad_logit.astype(jnp.bfloat16)
                key_sum[h, z] += dot(low, q_col[h])
                part = dot(key_rows[z, span[h], :], low)
                sums[h] = part if z == 0 else sums[h] + part
            total = total.astype(jnp.bfloat16)
            select_grad = running[z] + dot(total, later)
            running[z] = running[z] + dot(total, every)
            first = dot(key_heads[TEAM_HEADS, z], q_row[TEAM_HEADS])
            live = first > 0.0
            if z == count - 1:
                live = live & (last < query_pos)
            low = jnp.where(live, select_grad, 0.0).astype(jnp.bfloat16)
            key_sum[TEAM_HEADS, z] += dot(low, q_col[TEAM_HEADS])
            part = dot(key_rows[z, span[TEAM_HEADS], :], low)
            sums[TEAM_HEADS] = part if z == 0 else sums[TEAM_HEADS] + part
        for h in range(TEAM_HEADS + 1):
            query_grad_ref[0, 0, span[h], :] = sums[h].astype(jnp.bfloat16)

    for count in range(1, TEAMS + 1):
        pl.when(active == count)(functools.partial(work, count))

    @pl.when(step == blocks - 1)
    def _():
        for h in range(TEAM_HEADS + 1):
            key_grad_ref[:, :, span[h]] = key_sum[h].astype(jnp.bfloat16)
        for h in range(TEAM_HEADS):
            value_grad_ref[:, :, span[h]] = value_sum[h].astype(jnp.bfloat16)
        for z in range(TEAMS):
            for copy in grad_copies(z, False):
                copy.wait_send()
        for n in range(len(plan)):
            own_copy(n).wait()
        for scope in ("lane", "team"):
            for copy in plan_copies(scope, False):
                copy.wait()
        for n in range(len(plan)):
            for j in range(reduced[n].shape[0]):
                reduced[n][j] = added([targets[n][k, j] for k in range(targets[n].shape[0])])


def attend_back(queries, grads, stats, carried, keys, values, halves, blocks, rows, collective):
    lanes = blocks // TEAMS
    plan = reduce_plan
    shapes = exchange_shapes(plan, halves)

    def place(step):
        i = blocks - 1 - step
        return (lax.rem(i, lanes), i // lanes, 0, 0)

    return pl.pallas_call(
        functools.partial(attend_back_body, blocks=blocks, rows=rows),
        grid=(blocks,),
        in_specs=[
            pl.BlockSpec((1, 1, rows, QUERY_WIDTH), place),
            pl.BlockSpec((TEAMS, rows, TEAM_WIDTH), lambda step: (0, 0, 0)),
            pl.BlockSpec((TEAMS, 8, rows), lambda step: (0, 0, 0)),
            pl.BlockSpec((1, TEAMS, rows, rows), lambda step: (blocks - 1 - step, 0, 0, 0)),
            pl.BlockSpec((TEAMS, rows, QUERY_WIDTH), lambda step: (0, 0, 0)),
            pl.BlockSpec((TEAMS, rows, TEAM_WIDTH), lambda step: (0, 0, 0)),
        ]
        + [pl.BlockSpec(memory_space=pl.ANY)] * 3,
        out_specs=[
            pl.BlockSpec((1, 1, QUERY_WIDTH, rows), place),
            pl.BlockSpec((TEAMS, rows, QUERY_WIDTH), lambda step: (0, 0, 0)),
            pl.BlockSpec((TEAMS, rows, TEAM_WIDTH), lambda step: (0, 0, 0)),
        ]
        + [pl.BlockSpec(x.shape[1:], lambda step: (0, 0, 0)) for x in shapes],
        out_shape=[
            jax.ShapeDtypeStruct((lanes, TEAMS, QUERY_WIDTH, rows), jnp.bfloat16),
            jax.ShapeDtypeStruct((TEAMS, rows, QUERY_WIDTH), jnp.bfloat16),
            jax.ShapeDtypeStruct((TEAMS, rows, TEAM_WIDTH), jnp.bfloat16),
        ]
        + [jax.ShapeDtypeStruct(x.shape[1:], x.dtype) for x in shapes],
        scratch_shapes=[
            pltpu.VMEM((TEAM_HEADS + 1, TEAMS, rows, HEAD_DIM), jnp.bfloat16),
            pltpu.VMEM((TEAMS, QUERY_WIDTH, rows), jnp.bfloat16),
            pltpu.VMEM((TEAM_HEADS, TEAMS, rows, HEAD_DIM), jnp.bfloat16),
            pltpu.VMEM((TEAMS, rows, rows), jnp.float32),
            pltpu.VMEM((TEAM_HEADS + 1, TEAMS, rows, HEAD_DIM), jnp.float32),
            pltpu.VMEM((TEAM_HEADS, TEAMS, rows, HEAD_DIM), jnp.float32),
            pltpu.VMEM((lanes, TEAMS, rows, TEAM_WIDTH), jnp.bfloat16),
            pltpu.VMEM((lanes, TEAMS, 8, rows), jnp.float32),
            pltpu.SemaphoreType.DMA((2, TEAMS, lanes)),
            pltpu.SemaphoreType.DMA((2, TEAMS, lanes)),
        ]
        + exchange_sems(plan)
        + [pltpu.VMEM(x.shape, x.dtype) for x in shapes],
        compiler_params=pltpu.CompilerParams(
            collective_id=collective, has_side_effects=True, vmem_limit_bytes=VMEM_BYTES
        ),
    )(queries, grads, stats, carried, keys, values, *halves)


def finish_body(
    query_ref,
    key_ref,
    value_ref,
    lane_ref,
    weight_ref,
    gain_ref,
    bias_ref,
    base_ref,
    down_in,
    up_in,
    out_in,
    whole_ref,
    home_ref,
    total_ref,
    whole_down,
    whole_up,
    whole_out,
    query_parts,
    down_parts,
    up_parts,
    out_parts,
    down_ref,
    up_ref,
    out_ref,
    turned,
    weight_rows,
    weight_grad,
    rows_sum,
    rows_ref,
    main_ref,
    vector_ref,
    core_main,
    send_main,
    lane_main,
    team_send_main,
    team_main,
    assembled,
    vectors,
    ready,
    core_sems,
    lane_sems,
    team_sems,
    home_sems,
    vector_sems,
    out_lane_sems,
    out_core_sems,
    local_sems,
    early_team,
    early_lane,
    early_core,
    early_local,
    first_send,
    first_recv,
    first_local,
):
    lanes = lax.axis_size("seq") // TEAMS
    me = lax.axis_index("seq")
    core = lax.axis_index("batch")
    team, lane = me // lanes, lax.rem(me, lanes)

    def lane_peer(k):
        other = lax.rem(lane + k, lanes)
        return other, {"seq": team * lanes + other}

    def team_peer(k):
        other = lax.rem(team + k, TEAMS)
        return other, {"seq": other * lanes + lane}

    sibling = {"batch": 1 - core}
    greet(["core", "team", "lane"])
    first_sources = (query_ref, down_in, up_in, out_in)
    first_targets = (query_parts, down_parts, up_parts, out_parts)
    first_plan = [("team", "spread"), ("team", "spread"), ("lane", "spread"), ("lane", "spread")]
    first_copies = [[], []]
    for n in (1, 2, 3, 0):
        mine = peers_of(first_plan[n][0])[0]
        own = pltpu.make_async_copy(first_sources[n].at[mine], first_targets[n].at[mine], first_local.at[n])
        own.start()
        first_copies[n == 0].append(own)
        first_copies[n == 0] += remote_copies(
            first_plan[n : n + 1],
            first_sources[n : n + 1],
            first_targets[n : n + 1],
            first_send.at[n : n + 1],
            first_recv.at[n : n + 1],
        )
    spans = (slice(0, QUERY_WIDTH), slice(QUERY_WIDTH, 2 * QUERY_WIDTH), slice(2 * QUERY_WIDTH, None))
    for span in spans:
        weight_rows[span, :] = weight_ref[:, span].T
    weight_grad[...] = jnp.zeros_like(weight_grad)

    def known(b, _):
        rows_low = lane_ref[b].T
        turned[b] = rows_low
        total = None
        for span, grads in ((spans[1], key_ref[b]), (spans[2], value_ref[b])):
            weight_grad[:, span] += dot(rows_low, grads)
            part = dot(grads, weight_rows[span, :])
            total = part if total is None else total + part
        rows_sum[b] = total
        return 0

    lax.fori_loop(0, TEAMS, known, 0)
    for copy in first_copies[0]:
        copy.wait()
    down_ref[...] = added([down_parts[k] for k in range(lanes)])
    up_ref[...] = added([up_parts[k] for k in range(TEAMS)])
    out_ref[...] = added([out_parts[k] for k in range(TEAMS)])

    def place(n, p, t):
        if n == 0:
            return whole_down.at[core, p, t]
        ref = (None, whole_up, whole_out)[n]
        half = ref.shape[3] // 2
        return ref.at[p, t, :, pl.ds(pl.multiple_of(core * half, 128), half)]

    early = (down_ref, up_ref, out_ref)
    number = len(early)
    early_z = [[None] * TEAMS for _ in range(number)]
    for k in range(1, TEAMS):
        _, target = team_peer(k)
        for n in range(number):
            early_z[n][k] = push(
                early[n],
                place(n, lane, team),
                early_team.at[0, n, k],
                early_team.at[1, n, k],
                target,
            )
    early_kept = []
    for n in range(number):
        copy = pltpu.make_async_copy(early[n], place(n, lane, team), early_local.at[n])
        copy.start()
        early_kept.append(copy)
    early_out = []
    early_sib = []

    def forward(j):
        t = lax.rem(team - j + TEAMS, TEAMS)
        for n in range(number):
            if j == 0:
                source = early[n]
            else:
                early_z[n][j].wait_recv()
                source = place(n, lane, t)
            for k in range(1, lanes):
                _, target = lane_peer(k)
                early_out.append(
                    push(
                        source,
                        place(n, lane, t),
                        early_lane.at[0, n, j, k],
                        early_lane.at[1, n, j, k],
                        target,
                    )
                )
            early_sib.append(
                push(
                    source,
                    place(n, lane, t),
                    early_core.at[0, n, j, 0],
                    early_core.at[1, n, j, 0],
                    sibling,
                )
            )

    forward(0)
    for copy in first_copies[1]:
        copy.wait()
    gain = gain_ref[...]
    bias = bias_ref[...]

    def last(b, sums):
        query_rows = query_parts[0, b].astype(jnp.float32)
        for p in range(1, lanes):
            query_rows = query_rows + query_parts[p, b].astype(jnp.float32)
        grads = (query_rows * HEAD_DIM ** (-0.5)).astype(jnp.bfloat16).T
        weight_grad[:, spans[0]] += dot(turned[b], grads)
        total = rows_sum[b] + dot(grads, weight_rows[spans[0], :])
        rows_ref[b] = total.astype(jnp.bfloat16)
        shifted = lane_ref[b].astype(jnp.float32) - bias
        return (
            sums[0] + jnp.sum(total * shifted, axis=0, keepdims=True),
            sums[1] + jnp.sum(total, axis=0, keepdims=True),
        )

    nothing = jnp.zeros_like(gain)
    gain_sum, bias_sum = lax.fori_loop(0, TEAMS, last, (nothing, nothing))
    vector_ref[...] = base_ref[...]
    vector_ref[0:1, :] = gain_sum / gain
    vector_ref[1:2, :] = bias_sum
    depth = main_ref.shape[1]
    for chunk in range(2 * lanes):
        main_ref[chunk] = weight_grad[chunk * depth : (chunk + 1) * depth, :].astype(jnp.bfloat16)
    theirs = pl.ds((1 - core) * lanes, lanes)
    core_copies = [
        push(main_ref.at[theirs], core_main, core_sems.at[0, 0], core_sems.at[1, 0], sibling),
        push(vector_ref, vectors.at[0], vector_sems.at[0, 0], vector_sems.at[1, 0], sibling),
    ]
    for copy in core_copies:
        copy.wait()

    both = vector_ref[...] + vectors[0]
    vectors[1 + lane] = both
    ready[0] = both
    for j in range(lanes):
        send_main[j] = (
            main_ref[core * lanes + j].astype(jnp.float32) + core_main[j].astype(jnp.float32)
        ).astype(jnp.bfloat16)
    lane_copies = []
    for k in range(1, lanes):
        other, target = lane_peer(k)
        lane_copies += [
            push(send_main.at[other], lane_main.at[lane], lane_sems.at[0, 0, k], lane_sems.at[1, 0, k], target),
            push(ready.at[0], vectors.at[1 + lane], vector_sems.at[0, k], vector_sems.at[1, k], target),
        ]
    lane_main[lane] = send_main[lane]
    for copy in lane_copies:
        copy.wait()

    def total(ref, start, number):
        result = ref[start].astype(jnp.float32)
        for j in range(1, number):
            result = result + ref[start + j].astype(jnp.float32)
        return result

    whole_vector = total(vectors, 1, lanes)
    ready[1] = whole_vector
    vectors[1 + lanes + team] = whole_vector
    low_main = total(lane_main, 0, lanes).astype(jnp.bfloat16)
    team_send_main[...] = low_main
    team_main[team] = low_main
    team_copies = []
    for k in range(1, TEAMS):
        other, target = team_peer(k)
        at = lanes + k
        team_copies += [
            push(team_send_main, team_main.at[team], team_sems.at[0, 0, k], team_sems.at[1, 0, k], target),
            push(ready.at[1], vectors.at[1 + lanes + team], vector_sems.at[0, at], vector_sems.at[1, at], target),
        ]
    home_copies = []
    for k in range(1, TEAMS):
        other, target = team_peer(k)
        home_copies.append(
            push(rows_ref.at[other], home_ref.at[team], home_sems.at[0, k], home_sems.at[1, k], target)
        )
    own = pltpu.make_async_copy(rows_ref.at[team], home_ref.at[team], local_sems.at[0])
    own.start()
    for j in range(1, TEAMS):
        forward(j)
    for copy in team_copies:
        copy.wait()
    total_ref[...] = total(vectors, 1 + lanes, TEAMS)
    pieces = []
    for part in range(3):
        first = part * QUERY_WIDTH
        for g in range(TEAMS):
            piece = team_main[g, :, first : first + TEAM_WIDTH]
            if g == 0 and part < 2:
                more = piece[:, :HEAD_DIM].astype(jnp.float32)
                for other in range(TEAMS):
                    more = more + team_main[
                        other, :, first + TEAM_WIDTH : first + QUERY_WIDTH
                    ].astype(jnp.float32)
                pieces += [more.astype(jnp.bfloat16), piece[:, HEAD_DIM:]]
            else:
                pieces.append(piece)
    assembled[...] = jnp.concatenate(pieces, axis=1)

    mine = core * lanes + lane
    out_copies = []
    for k in range(1, lanes):
        _, target = lane_peer(k)
        out_copies.append(
            push(assembled, whole_ref.at[mine], out_lane_sems.at[0, k], out_lane_sems.at[1, k], target)
        )
    core_out = [
        push(assembled, whole_ref.at[mine], out_core_sems.at[0, 0], out_core_sems.at[1, 0], sibling)
    ]
    kept = pltpu.make_async_copy(assembled, whole_ref.at[mine], local_sems.at[1])
    kept.start()
    for j in range(TEAMS):
        for n in range(number):
            for k in range(1, lanes):
                early_out[(j * number + n) * (lanes - 1) + k - 1].wait_recv()
                p = lax.rem(lane - k + lanes, lanes)
                at = place(n, p, lax.rem(team - j + TEAMS, TEAMS))
                early_sib.append(
                    push(at, at, early_core.at[0, n, j, k], early_core.at[1, n, j, k], sibling)
                )
    for k in range(1, lanes):
        source = core * lanes + lax.rem(lane - k + lanes, lanes)
        out_copies[k - 1].wait_recv()
        core_out.append(
            push(
                whole_ref.at[source],
                whole_ref.at[source],
                out_core_sems.at[0, k],
                out_core_sems.at[1, k],
                sibling,
            )
        )
    for copy in out_copies + early_out:
        copy.wait_send()
    for n in range(number):
        for k in range(1, TEAMS):
            early_z[n][k].wait_send()
    for copy in core_out + home_copies + early_sib + early_kept:
        copy.wait()
    own.wait()
    kept.wait()


def finish(queries, keys, values, lane_rows, weight, gain, bias, base, reduced, collective):
    lanes = lax.axis_size("seq") // TEAMS
    width, columns = weight.shape
    rows = lane_rows.shape[1]
    chunks, depth = 2 * lanes, width // (2 * lanes)
    low = jnp.bfloat16
    dma = pltpu.SemaphoreType.DMA
    down, up, out = (x.shape[1:] for x in reduced)
    wholes = [
        (2, lanes, TEAMS) + down,
        (lanes, TEAMS, up[0], 2 * up[1]),
        (lanes, TEAMS, out[0], 2 * out[1]),
    ]
    anywhere = pl.BlockSpec(memory_space=pl.ANY)
    inside = pl.BlockSpec(memory_space=pltpu.VMEM)
    return pl.pallas_call(
        finish_body,
        out_shape=[
            jax.ShapeDtypeStruct((chunks, depth, 3 * width), low),
            jax.ShapeDtypeStruct(lane_rows.shape, low),
            jax.ShapeDtypeStruct(base.shape, jnp.float32),
        ]
        + [jax.ShapeDtypeStruct(shape, low) for shape in wholes],
        in_specs=[anywhere] + [inside] * 7 + [anywhere] * 3,
        out_specs=[anywhere, anywhere, inside] + [anywhere] * 3,
        scratch_shapes=[
            pltpu.VMEM(queries.shape, low),
            pltpu.VMEM((lanes,) + down, low),
            pltpu.VMEM((TEAMS,) + up, low),
            pltpu.VMEM((TEAMS,) + out, low),
            pltpu.VMEM(down, low),
            pltpu.VMEM(up, low),
            pltpu.VMEM(out, low),
            pltpu.VMEM((TEAMS, width, rows), low),
            pltpu.VMEM((columns, width), low),
            pltpu.VMEM((width, columns), jnp.float32),
            pltpu.VMEM((TEAMS, rows, width), jnp.float32),
            pltpu.VMEM((TEAMS, rows, width), low),
            pltpu.VMEM((chunks, depth, columns), low),
            pltpu.VMEM(base.shape, jnp.float32),
            pltpu.VMEM((lanes, depth, columns), low),
            pltpu.VMEM((lanes, depth, columns), low),
            pltpu.VMEM((lanes, depth, columns), low),
            pltpu.VMEM((depth, columns), low),
            pltpu.VMEM((TEAMS, depth, columns), low),
            pltpu.VMEM((depth, 3 * width), low),
            pltpu.VMEM((1 + lanes + TEAMS,) + base.shape, jnp.float32),
            pltpu.VMEM((2,) + base.shape, jnp.float32),
            dma((2, 2)),
            dma((2, 2, lanes)),
            dma((2, 2, TEAMS)),
            dma((2, TEAMS)),
            dma((2, lanes + TEAMS)),
            dma((2, lanes)),
            dma((2, lanes)),
            dma((2,)),
            dma((2, 3, TEAMS)),
            dma((2, 3, TEAMS, lanes)),
            dma((2, 3, TEAMS, lanes)),
            dma((3,)),
            dma((4, max(lanes, TEAMS))),
            dma((4, max(lanes, TEAMS))),
            dma((4,)),
        ],
        compiler_params=pltpu.CompilerParams(
            collective_id=collective, has_side_effects=True, vmem_limit_bytes=VMEM_BYTES
        ),
    )(queries, keys, values, lane_rows, weight, gain[None], bias[None], base, *reduced)


def contract_cols(left, right):
    return lax.dot_general(left, right, (((1,), (1,)), ((), ())), preferred_element_type=jnp.float32)


def dense_body(
    length_ref,
    mixed_ref,
    mass_ref,
    tokens_ref,
    grad_ref,
    gain_ref,
    bias_ref,
    w_out_hbm,
    w_up_hbm,
    w_down_hbm,
    layer_ref,
    resid_ref,
    norm_ref,
    cols_ref,
    stats_ref,
    down_hbm,
    up_hbm,
    out_hbm,
    w_out,
    w_up,
    w_down,
    active,
    slope,
    top,
    normed,
    mixed,
    slant,
    active_other,
    slope_other,
    top_other,
    normed_other,
    mixed_other,
    slant_other,
    total,
    back,
    cols,
    stats,
    down_half,
    up_half,
    out_half,
    load_sems,
    core_sems,
    lane_sems,
    keep_sems,
    store_sems,
):
    rows, width = tokens_ref.shape
    hidden = w_up.shape[1]
    step = width
    count = lax.axis_size("seq")
    lanes = count // TEAMS
    me = lax.axis_index("seq")
    core = lax.axis_index("batch")
    team, lane = me // lanes, lax.rem(me, lanes)
    sibling = {"batch": 1 - core}
    loads = [
        pltpu.make_async_copy(source, target, load_sems.at[n])
        for n, (source, target) in enumerate(
            ((w_out_hbm, w_out), (w_up_hbm, w_up), (w_down_hbm, w_down))
        )
    ]
    for load in loads:
        load.start()
    greet(["core", "lane"])

    def half_of(ref, which):
        half = ref.shape[1] // 2
        return ref.at[:, pl.ds(pl.multiple_of(which * half, 128), half)]

    pairs = (
        (active, active_other, True),
        (top, top_other, False),
        (normed, normed_other, False),
        (slope, slope_other, True),
        (mixed, mixed_other, False),
        (slant, slant_other, True),
    )

    def swap(n, start):
        source, target, halved = pairs[n]
        return push(
            half_of(source, 1 - core) if halved else source,
            target,
            core_sems.at[0, n],
            core_sems.at[1, n],
            sibling,
            start,
        )

    grad_top = grad_ref[...]
    top[...] = grad_top.astype(jnp.bfloat16)
    swap(1, True)
    valid = me * rows + lax.broadcasted_iota(jnp.int32, (rows, width), 0) < length_ref[0]
    mixed_rows = mixed_ref[...]
    mixed[...] = jnp.where(valid, mixed_rows.T, jnp.zeros((), jnp.bfloat16))
    swap(4, True)
    loads[0].wait()
    residual = tokens_ref[...] + dot(mixed[...], w_out[...])
    row_mean = jnp.mean(residual, axis=1, keepdims=True)
    centred = residual - row_mean
    variance = jnp.mean(centred * centred, axis=1, keepdims=True)
    spread = lax.rsqrt(variance + epsilon)
    scaled = centred * spread
    gain = gain_ref[...]
    normed[...] = (scaled * gain + bias_ref[...]).astype(jnp.bfloat16)
    swap(2, True)
    total[...] = residual
    back[...] = jnp.zeros_like(back)
    loads[1].wait()
    loads[2].wait()

    def chunk(c, _):
        at = pl.ds(pl.multiple_of(c * step, 128), step)
        up = w_up[:, at]
        down = w_down[at, :]
        u = dot(normed[...], up)
        squared = u * u
        bend = jnp.tanh(0.7978845608028654 * u * (1.0 + 0.044715 * squared))
        lift = 0.5 * (1.0 + bend)
        low = (u * lift).astype(jnp.bfloat16)
        active[:, at] = low
        turn = lift + (0.5 * 0.7978845608028654) * u * (1.0 - bend * bend) * (
            1.0 + (3.0 * 0.044715) * squared
        )
        grad_low = (contract_cols(top[...], down) * turn).astype(jnp.bfloat16)
        slope[:, at] = grad_low
        total[...] += dot(low, down)
        back[...] += contract_cols(grad_low, up)
        return 0

    lax.fori_loop(0, hidden // step, chunk, 0)
    swap(0, True)
    swap(3, True)
    layer_ref[...] = total[...]
    grad_normed = back[...]
    norm_ref[0:1, :] = jnp.sum(grad_normed * scaled, axis=0, keepdims=True)
    norm_ref[1:2, :] = jnp.sum(grad_normed, axis=0, keepdims=True)
    inner = grad_normed * gain
    resid = grad_top + spread * (
        inner
        - jnp.mean(inner, axis=1, keepdims=True)
        - scaled * jnp.mean(inner * scaled, axis=1, keepdims=True)
    )
    resid_ref[...] = resid
    slant[...] = resid.astype(jnp.bfloat16)
    swap(5, True)
    grad_mixed = contract_cols(slant[...], w_out[...]).astype(jnp.bfloat16)
    grad_mixed = jnp.where(valid, grad_mixed, jnp.zeros((), jnp.bfloat16))
    products = grad_mixed.T.astype(jnp.float32) * mixed_rows.astype(jnp.float32)
    for t in range(TEAMS):
        cols[t] = grad_mixed[:, t * TEAM_WIDTH : (t + 1) * TEAM_WIDTH]
        stats[t] = mass_ref[t]
        for h in range(TEAM_HEADS):
            first = t * TEAM_WIDTH + h * HEAD_DIM
            stats[t, TEAM_HEADS + h : TEAM_HEADS + h + 1, :] = jnp.sum(
                products[first : first + HEAD_DIM], axis=0, keepdims=True
            )
    copies = []
    for k in range(1, TEAMS):
        other = lax.rem(team + k, TEAMS)
        for n, (source, target) in enumerate(((cols, cols_ref), (stats, stats_ref))):
            copies.append(
                push(
                    source.at[other],
                    target.at[team],
                    lane_sems.at[0, n, k],
                    lane_sems.at[1, n, k],
                    {"seq": other * lanes + lane},
                )
            )
    for n, (source, target) in enumerate(((cols, cols_ref), (stats, stats_ref))):
        copy = pltpu.make_async_copy(source.at[team], target.at[team], keep_sems.at[n])
        copy.start()
        copies.append(copy)

    def pair_dot(left, left_other, right, right_other, at):
        return (
            dot(left[:, at].T, right[...]) + dot(left_other[:, at].T, right_other[...])
        ).astype(jnp.bfloat16)

    for n in range(len(pairs)):
        swap(n, False).wait()
    block = 384
    own_active = half_of(active, core)
    own_slope = half_of(slope, core)
    own_slant = half_of(slant, core)

    def down_rows(c, _):
        at = pl.ds(pl.multiple_of(c * block, 128), block)
        down_half[at, :] = pair_dot(own_active, active_other, top, top_other, at)
        return 0

    lax.fori_loop(0, down_half.shape[0] // block, down_rows, 0)
    stores = [pltpu.make_async_copy(down_half, down_hbm, store_sems.at[0])]
    stores[0].start()

    def up_rows(c, _):
        at = pl.ds(pl.multiple_of(c * block, 128), block)
        up_half[at, :] = pair_dot(normed, normed_other, own_slope, slope_other, at)
        out_half[at, :] = pair_dot(mixed, mixed_other, own_slant, slant_other, at)
        return 0

    lax.fori_loop(0, width // block, up_rows, 0)
    for n, (source, target) in enumerate(((up_half, up_hbm), (out_half, out_hbm))):
        copy = pltpu.make_async_copy(source, target, store_sems.at[1 + n])
        copy.start()
        stores.append(copy)
    for copy in copies + stores:
        copy.wait()


def dense(length, mixed, masses, tokens, grad, gain, bias, w_out, w_up, w_down, collective):
    rows, width = tokens.shape
    hidden = w_up.shape[1]
    low, full = jnp.bfloat16, jnp.float32
    inside = pl.BlockSpec(memory_space=pltpu.VMEM)
    anywhere = pl.BlockSpec(memory_space=pl.ANY)
    dma = pltpu.SemaphoreType.DMA
    half = hidden // 2
    return pl.pallas_call(
        dense_body,
        out_shape=[
            jax.ShapeDtypeStruct((rows, width), full),
            jax.ShapeDtypeStruct((rows, width), full),
            jax.ShapeDtypeStruct((2, width), full),
            jax.ShapeDtypeStruct((TEAMS, rows, TEAM_WIDTH), low),
            jax.ShapeDtypeStruct((TEAMS, 8, rows), full),
            jax.ShapeDtypeStruct((half, width), low),
            jax.ShapeDtypeStruct((width, half), low),
            jax.ShapeDtypeStruct((width, width // 2), low),
        ],
        in_specs=[pl.BlockSpec(memory_space=pltpu.SMEM)] + [inside] * 6 + [anywhere] * 3,
        out_specs=[inside] * 3 + [anywhere] * 5,
        scratch_shapes=[
            pltpu.VMEM((width, width), low),
            pltpu.VMEM((width, hidden), low),
            pltpu.VMEM((hidden, width), low),
            pltpu.VMEM((rows, hidden), low),
            pltpu.VMEM((rows, hidden), low),
            pltpu.VMEM((rows, width), low),
            pltpu.VMEM((rows, width), low),
            pltpu.VMEM((rows, width), low),
            pltpu.VMEM((rows, width), low),
            pltpu.VMEM((rows, half), low),
            pltpu.VMEM((rows, half), low),
            pltpu.VMEM((rows, width), low),
            pltpu.VMEM((rows, width), low),
            pltpu.VMEM((rows, width), low),
            pltpu.VMEM((rows, width // 2), low),
            pltpu.VMEM((rows, width), full),
            pltpu.VMEM((rows, width), full),
            pltpu.VMEM((TEAMS, rows, TEAM_WIDTH), low),
            pltpu.VMEM((TEAMS, 8, rows), full),
            pltpu.VMEM((half, width), low),
            pltpu.VMEM((width, half), low),
            pltpu.VMEM((width, width // 2), low),
            dma((3,)),
            dma((2, 6)),
            dma((2, 2, TEAMS)),
            dma((2,)),
            dma((3,)),
        ],
        compiler_params=pltpu.CompilerParams(
            collective_id=collective, has_side_effects=True, vmem_limit_bytes=VMEM_BYTES
        ),
    )(length, mixed, masses, tokens, grad, gain[None], bias[None], w_out, w_up, w_down)


def layer_norm(values, norm_gain, norm_bias):
    row_mean = jnp.mean(values, axis=-1, keepdims=True)
    centred = values - row_mean
    variance = jnp.mean(centred * centred, axis=-1, keepdims=True)
    return centred * lax.rsqrt(variance + epsilon) * norm_gain + norm_bias


def per_device(
    block_input,
    ln1_gain,
    ln1_bias,
    w_qkv,
    w_out,
    ln2_gain,
    ln2_bias,
    w_up,
    w_down,
    length_draw,
    threshold_index,
    grad_out,
):
    rows = block_input.shape[1]
    width = block_input.shape[2]
    blocks = lax.axis_size("seq")
    lanes = blocks // TEAMS
    group_len = blocks * rows
    me = lax.axis_index("seq")
    team = me // lanes
    length = group_len - rows + 1 + length_draw % rows
    threshold = threshold_index.astype(jnp.float32) / 128.0
    tokens = block_input[0]
    grad_top = grad_out[0]

    ln1_pull = jax.vjp(layer_norm, tokens, ln1_gain, ln1_bias)[1]
    lane_rows, team_weight, queries, keys, values = project(tokens, ln1_gain, ln1_bias, w_qkv, 0)

    head_out, masses, carried, excess = attend(
        length, threshold, queries, keys, values, blocks, rows, 1
    )
    layer_out, grad_resid, grad_ln2, grad_cols, stats, down_half, up_half, out_half = dense(
        length,
        head_out.reshape(width, rows),
        masses,
        tokens,
        grad_top,
        ln2_gain,
        ln2_bias,
        w_out,
        w_up,
        w_down,
        3,
    )
    halves = [x.reshape(lanes, TEAMS, -1, x.shape[1]) for x in (down_half, up_half, out_half)]
    query_grads, key_grads, value_grads, *halves = attend_back(
        queries, grad_cols, stats, carried, keys, values, halves, blocks, rows, 7
    )

    pairs = (length[0] - 1).astype(jnp.float32) * (length[0] - 2).astype(jnp.float32) / 2.0
    nothing = jnp.zeros((width,), jnp.float32)
    base = jnp.stack(
        [
            nothing,
            nothing,
            grad_ln2[0],
            grad_ln2[1],
            jnp.full((width,), jnp.sum(excess)),
            jnp.full((width,), pairs / blocks),
            nothing,
            nothing,
        ]
    )
    grad_w_qkv, home_rows, vectors, grad_w_down, grad_w_up, grad_w_out = finish(
        query_grads,
        key_grads,
        value_grads,
        lane_rows,
        team_weight,
        ln1_gain,
        ln1_bias,
        base,
        halves,
        6,
    )
    grad_w_down = grad_w_down.reshape(w_down.shape)
    grad_w_up = grad_w_up.reshape(w_up.shape)
    grad_w_out = grad_w_out.reshape(w_out.shape)
    grad_w_qkv = grad_w_qkv.reshape(width, 3 * width)
    grad_normed = jnp.sum(home_rows.astype(jnp.float32), axis=0)
    grad_x = grad_resid + ln1_pull(grad_normed)[0]
    pruned_share = (vectors[4, 0] / vectors[5, 0]).reshape(1)
    return (
        layer_out[None],
        grad_x[None],
        vectors[0],
        vectors[1],
        grad_w_qkv.astype(jnp.float32),
        grad_w_out.astype(jnp.float32),
        vectors[2],
        vectors[3],
        grad_w_up.astype(jnp.float32),
        grad_w_down.astype(jnp.float32),
        pruned_share,
    )


def solution(mesh):
    placed = (
        P("batch", "seq", None),
        P(),
        P(),
        P(),
        P(),
        P(),
        P(),
        P(),
        P(),
        P("batch"),
        P(),
        P("batch", "seq", None),
    )
    return jax.shard_map(
        per_device,
        mesh=mesh,
        in_specs=placed,
        out_specs=(
            P("batch", "seq", None),
            P("batch", "seq", None),
            P(),
            P(),
            P(),
            P(),
            P(),
            P(),
            P(),
            P(),
            P(),
        ),
        check_vma=False,
    )
```

profile of v0, /device:TPU:0, one launch (start us, length us, event | category | flops | bytes accessed | tf_op | source)
XLA Modules:
  0.0 329.1 jit_solution(13496737292578547921)
XLA Ops:
  1.3 1.3 broadcast_in_dim.29.gain_ref
  2.6 1.3 broadcast_in_dim.30.bias_ref
  3.8 42.9 %shard_map.203 = (bf16[4,256,768]{2,1,0:T(8,128)(2,1)}, bf16[768,704]{1,0:T(8,128)(2,1)}, bf16[4,4,256,256]{3,2,1,0:T(8,128)(2,1)}, bf16[4,256,256]{2,1,0:T(8,128)(2,1)}, bf16[4,256,192]{2,1,0:T(8,128)(2,1)}) custom-call(f32[256,768]{1,0:T(8,128)} %bitcast.27, f32[1,768]{1,0:T(1,128)} %broadcast_in_dim.29.gain_ref, f32[1,768]{1,0:T(1,128)} %broadcast_in_dim.30.bias_ref, ...), custom_call_target="tpu_custom_call" | custom-call | tf_op jit(solution)/shard_map/pallas_call | solution.py:321
  47.4 34.4 %shard_map.204 = (bf16[4,192,256]{2,1,0:T(8,128)(2,1)}, f32[4,8,256]{2,1,0:T(8,128)}, f32[16,4,256,256]{3,2,1,0:T(8,128)}, f32[8,256]{1,0:T(8,128)}) custom-call(s32[1]{0:T(128)S(6)} %add.34.length_ref, f32[1]{0:T(128)S(6)} %div.31.threshold_ref, bf16[4,4,256,256]{3,2,1,0:T(8,128)(2,1)} %get-tuple-element.40.q_ref, ...), custom_call_target="tpu_custom_call" | custom-call | tf_op jit(solution)/shard_map/pallas_call | solution.py:580
  81.8 0.0 copy-done.10
  81.9 0.6 broadcast_in_dim.31.gain_ref
  82.4 0.0 copy-done.11
  82.4 0.6 broadcast_in_dim.32.bias_ref
  83.0 26.3 %shard_map.205 = (f32[256,768]{1,0:T(8,128)}, f32[256,768]{1,0:T(8,128)}, f32[2,768]{1,0:T(2,128)}, bf16[4,256,192]{2,1,0:T(8,128)(2,1)}, f32[4,8,256]{2,1,0:T(8...) custom-call(s32[1]{0:T(128)S(6)} %add.34.length_ref, ...), custom_call_target="tpu_custom_call" | custom-call | tf_op jit(solution)/shard_map/pallas_call | solution.py:1464
  109.4 0.0 copy-done.8
  109.4 0.6 reduce_sum.51
  110.0 0.6 stack_broadcast_in_dim.6
  110.6 1.3 stack.3.base_ref
  112.0 66.0 %shard_map.206 = (bf16[4,4,256,256]{3,2,1,0:T(8,128)(2,1)}, bf16[4,256,256]{2,1,0:T(8,128)(2,1)}, bf16[4,256,192]{2,1,0:T(8,128)(2,1)}, bf16[4,96,768]{2,1,0:T(8...) custom-call(bf16[4,4,256,256]{3,2,1,0:T(8,128)(2,1)} %get-tuple-element.40.q_ref, ...), custom_call_target="tpu_custom_call" | custom-call | tf_op jit(solution)/shard_map/pallas_call | solution.py:812
  178.0 126.0 %shard_map.207 = (bf16[8,96,2304]{2,1,0:T(8,128)(2,1)}, bf16[4,256,768]{2,1,0:T(8,128)(2,1)}, f32[8,768]{1,0:T(8,128)}, bf16[2,4,4,96,768]{4,3,2,1,0:T(8,128)(2,...) custom-call(bf16[4,4,256,256]{3,2,1,0:T(8,128)(2,1)} %get-tuple-element.53.query_ref, ...), custom_call_target="tpu_custom_call" | custom-call | tf_op jit(solution)/shard_map/pallas_call | solution.py:1185
  304.0 1.3 fusion.2
  306.6 0.0 copy-start.1
  306.6 7.0 %bitcast_convert_fusion = f32[3072,768]{1,0:T(8,128)} fusion(bf16[2,4,4,96,768]{4,3,2,1,0:T(8,128)(2,1)} %get-tuple-element.68), kind=kLoop, calls=%fused_computation | loop fusion | flops 2359296 | bytes 14155776 | tf_op jit(solution)/shard_map/convert_element_type | solution.py:1613
  313.6 5.3 %bitcast_convert_fusion.1 = f32[768,3072]{1,0:T(8,128)} fusion(bf16[4,4,48,3072]{3,2,1,0:T(8,128)(2,1)S(1)} %copy-done.1), kind=kLoop, calls=%fused_computation.1 | loop fusion | flops 2359296 | bytes 14155776 | tf_op jit(solution)/shard_map/convert_element_type | solution.py:1612
  319.0 3.7 %bitcast_convert_fusion.2 = f32[768,2304]{1,0:T(8,128)} fusion(bf16[8,96,2304]{2,1,0:T(8,128)(2,1)S(1)} %copy-done.2), kind=kLoop, calls=%fused_computation.2 | loop fusion | flops 1769472 | bytes 10616832 | tf_op jit(solution)/shard_map/convert_element_type | solution.py:1608
  322.7 0.2 convert_reduce_fusion
  322.9 0.1 reduce_sum.64
  323.1 0.3 multiply_reduce_fusion.1
  323.4 0.3 fusion.1
  323.7 0.0 copy-start.9
  323.7 0.0 copy-start.5
  323.8 0.1 copy-done.6
  323.8 1.0 add_bitcast_fusion
  324.8 0.0 copy-done.4
  324.8 1.7 bitcast_convert_fusion.3
  326.5 0.6 slice_reduce_fusion
  327.1 0.9 copy.26
  (21 shorter events, 0.1 us)
Async XLA Ops:
  3.8 78.0 %copy-start.10 = (f32[768]{0:T(1024)S(1)}, f32[768]{0:T(1024)}, u32[]{:S(2)}) copy-start(f32[768]{0:T(1024)} %param.17) | copy-start | bytes 9220
  3.8 78.6 %copy-start.11 = (f32[768]{0:T(1024)S(1)}, f32[768]{0:T(1024)}, u32[]{:S(2)}) copy-start(f32[768]{0:T(1024)} %param.18) | copy-start | bytes 9220
  83.0 26.3 %copy-start.8 = (f32[8,256]{1,0:T(8,128)S(1)}, f32[8,256]{1,0:T(8,128)}, u32[]{:S(2)}) copy-start(f32[8,256]{1,0:T(8,128)} %get-tuple-element.59) | copy-start | bytes 24580
  306.6 7.0 %copy-start.1 = (bf16[4,4,48,3072]{3,2,1,0:T(8,128)(2,1)S(1)}, bf16[4,4,48,3072]{3,2,1,0:T(8,128)(2,1)}, u32[]{:S(2)}) copy-start(bf16[4,4,48,3072]{3,2,1,0:T(8,128)(2,1)} %get-tuple-element.67) | copy-start | bytes 14155780
  313.6 5.3 %copy-start.2 = (bf16[8,96,2304]{2,1,0:T(8,128)(2,1)S(1)}, bf16[8,96,2304]{2,1,0:T(8,128)(2,1)}, u32[]{:S(2)}) copy-start(bf16[8,96,2304]{2,1,0:T(8,128)(2,1)} %get-tuple-element.65) | copy-start | bytes 10616836
  319.0 3.7 %copy-start.3 = (bf16[4,256,768]{2,1,0:T(8,128)(2,1)S(1)}, bf16[4,256,768]{2,1,0:T(8,128)(2,1)}, u32[]{:S(2)}) copy-start(bf16[4,256,768]{2,1,0:T(8,128)(2,1)} %get-tuple-element.63) | copy-start | bytes 4718596
  319.0 3.9 %copy-start = (f32[1,256,768]{2,1,0:T(8,128)S(1)}, f32[1,256,768]{2,1,0:T(8,128)}, u32[]{:S(2)}) copy-start(f32[1,256,768]{2,1,0:T(8,128)} %param.12) | copy-start | bytes 2359300
  319.0 4.1 %copy-start.7 = (f32[768]{0:T(1024)S(1)}, f32[768]{0:T(1024)}, u32[]{:S(2)}) copy-start(f32[768]{0:T(1024)} %param.13) | copy-start | bytes 9220
  322.7 1.1 copy-start.6
  322.9 1.9 copy-start.4
  323.7 2.8 copy-start.9
  323.7 3.4 %copy-start.5 = (f32[256,768]{1,0:T(8,128)S(1)}, f32[256,768]{1,0:T(8,128)}, u32[]{:S(2)}) copy-start(f32[256,768]{1,0:T(8,128)} %get-tuple-element.45) | copy-start | bytes 2359300
where the time goes:
time: 330 us; the launch traced here: 329 us
  Pallas kernels  296 us (90%)
  other arithmetic  20.3 us (6%)
  local copies, waits for them, and re-layouts  8.54 us (3%)
  between operations  4.6 us (1%)
    pallas_call x1, Pallas kernels, finish(): pl.pallas_call(finish_body, out_shape=[jax.ShapeDtypeStruct((chunks, dept...  126 us
    pallas_call x1, Pallas kernels, attend_back(): pl.pallas_call(functools.partial(attend_back_body, blocks=blocks, rows=ro...  66 us
    pallas_call x1, Pallas kernels, project(): pl.pallas_call(project_body, out_shape=[jax.ShapeDtypeStruct((TEAMS, rows...  42.9 us
    pallas_call x1, Pallas kernels, attend(): pl.pallas_call(functools.partial(attend_body, blocks=blocks, rows=rows),...  34.4 us
    pallas_call x1, Pallas kernels, dense(): pl.pallas_call(dense_body, out_shape=[jax.ShapeDtypeStruct((rows, width),...  26.3 us
    convert_element_type x1, other arithmetic, per_device(): grad_w_down.astype(jnp.float32)  6.97 us

commit v1 on v0

--- a/solution.py
+++ b/solution.py
@@ -206,7 +206,9 @@
     row_mean = jnp.mean(tokens, axis=1, keepdims=True)
     centred = tokens - row_mean
     variance = jnp.mean(centred * centred, axis=1, keepdims=True)
-    normed = centred * lax.rsqrt(variance + epsilon) * gain_ref[...] + bias_ref[...]
+    normed = (
+        centred * lax.rsqrt(variance + epsilon) * gain_ref[...][None, :] + bias_ref[...][None, :]
+    )
     held[team] = normed.astype(jnp.bfloat16)
     greet(["team", "lane"])
 
@@ -344,7 +346,7 @@
         compiler_params=pltpu.CompilerParams(
             collective_id=collective, has_side_effects=True, vmem_limit_bytes=VMEM_BYTES
         ),
-    )(tokens, gain[None], bias[None], weight)
+    )(tokens, gain, bias, weight)
 
 
 def fold(tile):
@@ -861,7 +863,9 @@
     weight_ref,
     gain_ref,
     bias_ref,
-    base_ref,
+    norm_ref,
+    excess_ref,
+    length_ref,
     down_in,
     up_in,
     out_in,
@@ -963,12 +967,33 @@
     up_ref[...] = added([up_parts[k] for k in range(TEAMS)])
     out_ref[...] = added([out_parts[k] for k in range(TEAMS)])
 
-    def place(n, p, t):
+    def place(n, p, t, part=None):
         if n == 0:
-            return whole_down.at[core, p, t]
-        ref = (None, whole_up, whole_out)[n]
-        half = ref.shape[3] // 2
-        return ref.at[p, t, :, pl.ds(pl.multiple_of(core * half, 128), half)]
+            ref, start, wide = whole_down.at[core, p, t], 0, whole_down.shape[4]
+        else:
+            ref = (None, whole_up, whole_out)[n]
+            wide = ref.shape[3] // 2
+            ref, start = ref.at[p, t], core * wide
+        cut = (wide // 128 + 1) // 2 * 128
+        if part is not None:
+            start, wide = ((start, cut), (start + cut, wide - cut))[part]
+        return ref.at[:, pl.ds(pl.multiple_of(start, 128), wide)]
+
+    square = lanes == 4
+    if square:
+        across, along = lax.rem(lane, 2), lane // 2
+        direct = [2 * along + 1 - across, 2 * (1 - along) + across]
+        origins = direct
+    else:
+        direct = [lax.rem(lane + k, lanes) for k in range(1, lanes)]
+        origins = [lax.rem(lane - k + lanes, lanes) for k in range(1, lanes)]
+    corner = lanes - 1 - lane
+
+    def lane_of(p):
+        return {"seq": team * lanes + p}
+
+    def landed(ref, sem):
+        pltpu.make_async_copy(ref, ref, sem).wait()
 
     early = (down_ref, up_ref, out_ref)
     number = len(early)
@@ -999,32 +1024,42 @@
             else:
                 early_z[n][j].wait_recv()
                 source = place(n, lane, t)
-            for k in range(1, lanes):
-                _, target = lane_peer(k)
-                early_out.append(
-                    push(
-                        source,
-                        place(n, lane, t),
-                        early_lane.at[0, n, j, k],
-                        early_lane.at[1, n, j, k],
-                        target,
-                    )
-                )
-            early_sib.append(
-                push(
-                    source,
-                    place(n, lane, t),
-                    early_core.at[0, n, j, 0],
-                    early_core.at[1, n, j, 0],
-                    sibling,
-                )
-            )
+            target = place(n, lane, t)
+            for m, p in enumerate(direct):
+                sems = [early_lane.at[side, n, j, m] for side in range(2)]
+                early_out.append(push(source, target, *sems, lane_of(p)))
+            sems = [early_core.at[side, n, j, 0] for side in range(2)]
+            early_sib.append(push(source, target, *sems, sibling))
+
+    def relay(j):
+        t = lax.rem(team - j + TEAMS, TEAMS)
+        for n in range(number):
+            for m, p in enumerate(origins):
+                piece = place(n, p, t)
+                landed(piece, early_lane.at[1, n, j, m])
+                if square:
+                    side = place(n, p, t, m)
+                    sems = [early_lane.at[side_, n, j, 2 + m] for side_ in range(2)]
+                    early_out.append(push(side, side, *sems, lane_of(direct[1 - m])))
+                sems = [early_core.at[side_, n, j, 1 + m] for side_ in range(2)]
+                early_sib.append(push(piece, piece, *sems, sibling))
+
+    def settle(j):
+        if not square:
+            return
+        t = lax.rem(team - j + TEAMS, TEAMS)
+        for n in range(number):
+            for m in range(2):
+                landed(place(n, corner, t, m), early_lane.at[1, n, j, 2 + m])
+            piece = place(n, corner, t)
+            sems = [early_core.at[side, n, j, 3] for side in range(2)]
+            early_sib.append(push(piece, piece, *sems, sibling))
 
     forward(0)
     for copy in first_copies[1]:
         copy.wait()
-    gain = gain_ref[...]
-    bias = bias_ref[...]
+    gain = gain_ref[...][None, :]
+    bias = bias_ref[...][None, :]
 
     def last(b, sums):
         query_rows = query_parts[0, b].astype(jnp.float32)
@@ -1042,9 +1077,15 @@
 
     nothing = jnp.zeros_like(gain)
     gain_sum, bias_sum = lax.fori_loop(0, TEAMS, last, (nothing, nothing))
-    vector_ref[...] = base_ref[...]
+    length = length_ref[0].astype(jnp.float32)
+    pairs = (length - 1.0) * (length - 2.0) / (2.0 * TEAMS * lanes)
+    excess = jnp.sum(jnp.sum(excess_ref[...], axis=0, keepdims=True), axis=1, keepdims=True)
+    vector_ref[...] = jnp.zeros_like(vector_ref)
     vector_ref[0:1, :] = gain_sum / gain
     vector_ref[1:2, :] = bias_sum
+    vector_ref[2:4, :] = norm_ref[...]
+    vector_ref[4:5, :] = jnp.broadcast_to(excess, nothing.shape)
+    vector_ref[5:6, :] = jnp.full(nothing.shape, pairs)
     depth = main_ref.shape[1]
     for chunk in range(2 * lanes):
         main_ref[chunk] = weight_grad[chunk * depth : (chunk + 1) * depth, :].astype(jnp.bfloat16)
@@ -1055,6 +1096,7 @@
     ]
     for copy in core_copies:
         copy.wait()
+    relay(0)
 
     both = vector_ref[...] + vectors[0]
     vectors[1 + lane] = both
@@ -1104,6 +1146,9 @@
     own.start()
     for j in range(1, TEAMS):
         forward(j)
+        settle(j - 1)
+        if j < TEAMS - 1:
+            relay(j)
     for copy in team_copies:
         copy.wait()
     total_ref[...] = total(vectors, 1 + lanes, TEAMS)
@@ -1123,39 +1168,33 @@
                 pieces.append(piece)
     assembled[...] = jnp.concatenate(pieces, axis=1)
 
-    mine = core * lanes + lane
-    out_copies = []
-    for k in range(1, lanes):
-        _, target = lane_peer(k)
-        out_copies.append(
-            push(assembled, whole_ref.at[mine], out_lane_sems.at[0, k], out_lane_sems.at[1, k], target)
-        )
-    core_out = [
-        push(assembled, whole_ref.at[mine], out_core_sems.at[0, 0], out_core_sems.at[1, 0], sibling)
-    ]
-    kept = pltpu.make_async_copy(assembled, whole_ref.at[mine], local_sems.at[1])
+    def chunk_of(p, part=None):
+        ref = whole_ref.at[core * lanes + p]
+        half = whole_ref.shape[2] // 2
+        return ref if part is None else ref.at[:, pl.ds(part * half, half)]
+
+    out_copies, core_out = [], []
+    for m, p in enumerate(direct):
+        sems = [out_lane_sems.at[side, m] for side in range(2)]
+        out_copies.append(push(assembled, chunk_of(lane), *sems, lane_of(p)))
+    sems = [out_core_sems.at[side, 0] for side in range(2)]
+    core_out.append(push(assembled, chunk_of(lane), *sems, sibling))
+    kept = pltpu.make_async_copy(assembled, chunk_of(lane), local_sems.at[1])
     kept.start()
-    for j in range(TEAMS):
-        for n in range(number):
-            for k in range(1, lanes):
-                early_out[(j * number + n) * (lanes - 1) + k - 1].wait_recv()
-                p = lax.rem(lane - k + lanes, lanes)
-                at = place(n, p, lax.rem(team - j + TEAMS, TEAMS))
-                early_sib.append(
-                    push(at, at, early_core.at[0, n, j, k], early_core.at[1, n, j, k], sibling)
-                )
-    for k in range(1, lanes):
-        source = core * lanes + lax.rem(lane - k + lanes, lanes)
-        out_copies[k - 1].wait_recv()
-        core_out.append(
-            push(
-                whole_ref.at[source],
-                whole_ref.at[source],
-                out_core_sems.at[0, k],
-                out_core_sems.at[1, k],
-                sibling,
-            )
-        )
+    relay(TEAMS - 1)
+    for m, p in enumerate(origins):
+        landed(chunk_of(p), out_lane_sems.at[1, m])
+        if square:
+            sems = [out_lane_sems.at[side, 2 + m] for side in range(2)]
+            out_copies.append(push(chunk_of(p, m), chunk_of(p, m), *sems, lane_of(direct[1 - m])))
+        sems = [out_core_sems.at[side, 1 + m] for side in range(2)]
+        core_out.append(push(chunk_of(p), chunk_of(p), *sems, sibling))
+    settle(TEAMS - 1)
+    if square:
+        for m in range(2):
+            landed(chunk_of(corner, m), out_lane_sems.at[1, 2 + m])
+        sems = [out_core_sems.at[side, 3] for side in range(2)]
+        core_out.append(push(chunk_of(corner), chunk_of(corner), *sems, sibling))
     for copy in out_copies + early_out:
         copy.wait_send()
     for n in range(number):
@@ -1167,10 +1206,13 @@
     kept.wait()
 
 
-def finish(queries, keys, values, lane_rows, weight, gain, bias, base, reduced, collective):
+def finish(
+    queries, keys, values, lane_rows, weight, gain, bias, norm, excess, length, reduced, collective
+):
     lanes = lax.axis_size("seq") // TEAMS
     width, columns = weight.shape
     rows = lane_rows.shape[1]
+    vector = (8, width)
     chunks, depth = 2 * lanes, width // (2 * lanes)
     low = jnp.bfloat16
     dma = pltpu.SemaphoreType.DMA
@@ -1187,10 +1229,13 @@
         out_shape=[
             jax.ShapeDtypeStruct((chunks, depth, 3 * width), low),
             jax.ShapeDtypeStruct(lane_rows.shape, low),
-            jax.ShapeDtypeStruct(base.shape, jnp.float32),
+            jax.ShapeDtypeStruct(vector, jnp.float32),
         ]
         + [jax.ShapeDtypeStruct(shape, low) for shape in wholes],
-        in_specs=[anywhere] + [inside] * 7 + [anywhere] * 3,
+        in_specs=[anywhere]
+        + [inside] * 8
+        + [pl.BlockSpec(memory_space=pltpu.SMEM)]
+        + [anywhere] * 3,
         out_specs=[anywhere, anywhere, inside] + [anywhere] * 3,
         scratch_shapes=[
             pltpu.VMEM(queries.shape, low),
@@ -1206,15 +1251,15 @@
             pltpu.VMEM((TEAMS, rows, width), jnp.float32),
             pltpu.VMEM((TEAMS, rows, width), low),
             pltpu.VMEM((chunks, depth, columns), low),
-            pltpu.VMEM(base.shape, jnp.float32),
+            pltpu.VMEM(vector, jnp.float32),
             pltpu.VMEM((lanes, depth, columns), low),
             pltpu.VMEM((lanes, depth, columns), low),
             pltpu.VMEM((lanes, depth, columns), low),
             pltpu.VMEM((depth, columns), low),
             pltpu.VMEM((TEAMS, depth, columns), low),
             pltpu.VMEM((depth, 3 * width), low),
-            pltpu.VMEM((1 + lanes + TEAMS,) + base.shape, jnp.float32),
-            pltpu.VMEM((2,) + base.shape, jnp.float32),
+            pltpu.VMEM((1 + lanes + TEAMS,) + vector, jnp.float32),
+            pltpu.VMEM((2,) + vector, jnp.float32),
             dma((2, 2)),
             dma((2, 2, lanes)),
             dma((2, 2, TEAMS)),
@@ -1234,7 +1279,7 @@
         compiler_params=pltpu.CompilerParams(
             collective_id=collective, has_side_effects=True, vmem_limit_bytes=VMEM_BYTES
         ),
-    )(queries, keys, values, lane_rows, weight, gain[None], bias[None], base, *reduced)
+    )(queries, keys, values, lane_rows, weight, gain, bias, norm, excess, length, *reduced)
 
 
 def contract_cols(left, right):
@@ -1345,8 +1390,8 @@
     variance = jnp.mean(centred * centred, axis=1, keepdims=True)
     spread = lax.rsqrt(variance + epsilon)
     scaled = centred * spread
-    gain = gain_ref[...]
-    normed[...] = (scaled * gain + bias_ref[...]).astype(jnp.bfloat16)
+    gain = gain_ref[...][None, :]
+    normed[...] = (scaled * gain + bias_ref[...][None, :]).astype(jnp.bfloat16)
     swap(2, True)
     total[...] = residual
     back[...] = jnp.zeros_like(back)
@@ -1507,14 +1552,49 @@
         compiler_params=pltpu.CompilerParams(
             collective_id=collective, has_side_effects=True, vmem_limit_bytes=VMEM_BYTES
         ),
-    )(length, mixed, masses, tokens, grad, gain[None], bias[None], w_out, w_up, w_down)
-
-
-def layer_norm(values, norm_gain, norm_bias):
-    row_mean = jnp.mean(values, axis=-1, keepdims=True)
-    centred = values - row_mean
-    variance = jnp.mean(centred * centred, axis=-1, keepdims=True)
-    return centred * lax.rsqrt(variance + epsilon) * norm_gain + norm_bias
+    )(length, mixed, masses, tokens, grad, gain, bias, w_out, w_up, w_down)
+
+
+def close_body(tokens_ref, gain_ref, resid_ref, home_ref, *refs):
+    grad_ref, rest = refs[len(refs) // 2], refs[: len(refs) // 2] + refs[len(refs) // 2 + 1 :]
+    for n in range(len(rest) // 2):
+        rest[len(rest) // 2 + n][...] = rest[n][...].astype(jnp.float32)
+    tokens = tokens_ref[...]
+    centred = tokens - jnp.mean(tokens, axis=1, keepdims=True)
+    spread = lax.rsqrt(jnp.mean(centred * centred, axis=1, keepdims=True) + epsilon)
+    scaled = centred * spread
+    total = home_ref[0].astype(jnp.float32)
+    for t in range(1, TEAMS):
+        total = total + home_ref[t].astype(jnp.float32)
+    inner = total * gain_ref[...][None, :]
+    grad_ref[...] = resid_ref[...] + spread * (
+        inner
+        - jnp.mean(inner, axis=1, keepdims=True)
+        - scaled * jnp.mean(inner * scaled, axis=1, keepdims=True)
+    )
+
+
+def close(tokens, gain, resid, home, weights):
+    steps = 8
+    rows, width = tokens.shape
+
+    def band(x):
+        return pl.BlockSpec((x.shape[0] // steps, x.shape[1]), lambda i: (i, 0))
+
+    return pl.pallas_call(
+        close_body,
+        grid=(steps,),
+        in_specs=[
+            band(tokens),
+            pl.BlockSpec((width,), lambda i: (0,)),
+            band(resid),
+            pl.BlockSpec((TEAMS, rows // steps, width), lambda i: (0, i, 0)),
+        ]
+        + [band(x) for x in weights],
+        out_specs=[band(tokens)] + [band(x) for x in weights],
+        out_shape=[jax.ShapeDtypeStruct(x.shape, jnp.float32) for x in [tokens] + weights],
+        compiler_params=pltpu.CompilerParams(vmem_limit_bytes=VMEM_BYTES),
+    )(tokens, gain, resid, home, *weights)
 
 
 def per_device(
@@ -1543,7 +1623,6 @@
     tokens = block_input[0]
     grad_top = grad_out[0]
 
-    ln1_pull = jax.vjp(layer_norm, tokens, ln1_gain, ln1_bias)[1]
     lane_rows, team_weight, queries, keys, values = project(tokens, ln1_gain, ln1_bias, w_qkv, 0)
 
     head_out, masses, carried, excess = attend(
@@ -1567,20 +1646,6 @@
         queries, grad_cols, stats, carried, keys, values, halves, blocks, rows, 7
     )
 
-    pairs = (length[0] - 1).astype(jnp.float32) * (length[0] - 2).astype(jnp.float32) / 2.0
-    nothing = jnp.zeros((width,), jnp.float32)
-    base = jnp.stack(
-        [
-            nothing,
-            nothing,
-            grad_ln2[0],
-            grad_ln2[1],
-            jnp.full((width,), jnp.sum(excess)),
-            jnp.full((width,), pairs / blocks),
-            nothing,
-            nothing,
-        ]
-    )
     grad_w_qkv, home_rows, vectors, grad_w_down, grad_w_up, grad_w_out = finish(
         query_grads,
         key_grads,
@@ -1589,28 +1654,36 @@
         team_weight,
         ln1_gain,
         ln1_bias,
-        base,
+        grad_ln2,
+        excess,
+        length,
         halves,
         6,
     )
-    grad_w_down = grad_w_down.reshape(w_down.shape)
-    grad_w_up = grad_w_up.reshape(w_up.shape)
-    grad_w_out = grad_w_out.reshape(w_out.shape)
-    grad_w_qkv = grad_w_qkv.reshape(width, 3 * width)
-    grad_normed = jnp.sum(home_rows.astype(jnp.float32), axis=0)
-    grad_x = grad_resid + ln1_pull(grad_normed)[0]
+    grad_x, grad_w_qkv, grad_w_out, grad_w_up, grad_w_down = close(
+        tokens,
+        ln1_gain,
+        grad_resid,
+        home_rows,
+        [
+            grad_w_qkv.reshape(w_qkv.shape),
+            grad_w_out.reshape(w_out.shape),
+            grad_w_up.reshape(w_up.shape),
+            grad_w_down.reshape(w_down.shape),
+        ],
+    )
     pruned_share = (vectors[4, 0] / vectors[5, 0]).reshape(1)
     return (
         layer_out[None],
         grad_x[None],
         vectors[0],
         vectors[1],
-        grad_w_qkv.astype(jnp.float32),
-        grad_w_out.astype(jnp.float32),
+        grad_w_qkv,
+        grad_w_out,
         vectors[2],
         vectors[3],
-        grad_w_up.astype(jnp.float32),
-        grad_w_down.astype(jnp.float32),
+        grad_w_up,
+        grad_w_down,
         pruned_share,
     )
 

time: 330 us -> 306 us (0.927)
  other arithmetic: 20.3 us -> 0 us
  local copies, waits for them, and re-layouts: 8.54 us -> 3.67 us
    pallas_call x1, Pallas kernels: 126 us -> 108 us  [finish(): pl.pallas_call(finish_body, out_shape=[jax.ShapeDtypeStruct((chunks, dept...]
    convert_element_type x4 -> x0, other arithmetic: 17.7 us -> none  [the longest x1 6.97 us: per_device(): grad_w_down.astype(jnp.float32)]
    pallas_call x0 -> x1, Pallas kernels: none -> 16.6 us  [close(): pl.pallas_call(close_body, grid=(steps,), in_specs=[band(tokens), pl.Bloc...]
    broadcast_in_dim x4 -> x0, local copies, waits for them, and re-layouts: 3.7 us -> none  [the longest x1 1.27 us: project(): gain[None]]
where the time goes in v1:
time: 306 us; the launch traced here: 302 us
  Pallas kernels  294 us (96%)
  between operations  4.47 us (1%)
  local copies, waits for them, and re-layouts  3.67 us (1%)
    pallas_call x1, Pallas kernels, finish(): pl.pallas_call(finish_body, out_shape=[jax.ShapeDtypeStruct((chunks, dept...  108 us
    pallas_call x1, Pallas kernels, attend_back(): pl.pallas_call(functools.partial(attend_back_body, blocks=blocks, rows=ro...  66.3 us
    pallas_call x1, Pallas kernels, project(): pl.pallas_call(project_body, out_shape=[jax.ShapeDtypeStruct((TEAMS, rows...  42.9 us
    pallas_call x1, Pallas kernels, attend(): pl.pallas_call(functools.partial(attend_body, blocks=blocks, rows=rows),...  34.4 us
    pallas_call x1, Pallas kernels, dense(): pl.pallas_call(dense_body, out_shape=[jax.ShapeDtypeStruct((rows, width),...  26.3 us
    pallas_call x1, Pallas kernels, close(): pl.pallas_call(close_body, grid=(steps,), in_specs=[band(tokens), pl.Bloc...  16.6 us

profile of v1, /device:TPU:0, one launch (start us, length us, event | category | flops | bytes accessed | tf_op | source)
XLA Modules:
  0.0 302.4 jit_solution(2346014467063542918)
XLA Ops:
  2.0 42.9 %shard_map.203 = (bf16[4,256,768]{2,1,0:T(8,128)(2,1)}, bf16[768,704]{1,0:T(8,128)(2,1)}, bf16[4,4,256,256]{3,2,1,0:T(8,128)(2,1)}, bf16[4,256,256]{2,1,0:T(8,128)(2,1)}, bf16[4,256,192]{2,1,0:T(8,128)(2,1)}) custom-call(f32[256,768]{1,0:T(8,128)} %bitcast.13, f32[768]{0:T(1024)} %gain_ref.7, f32[768]{0:T(1024)} %bias_ref.5, bf16[768,2304]{1,0:T(8,128)(2,1)} %w_ref.1), custom_call_target="tpu_custom_call" | custom-call | tf_op jit(solution)/shard_map/pallas_call | solution.py:323
  44.8 34.4 %shard_map.204 = (bf16[4,192,256]{2,1,0:T(8,128)(2,1)}, f32[4,8,256]{2,1,0:T(8,128)}, f32[16,4,256,256]{3,2,1,0:T(8,128)}, f32[8,256]{1,0:T(8,128)}) custom-call(s32[1]{0:T(128)S(6)} %add.10.length_ref, f32[1]{0:T(128)S(6)} %div.7.threshold_ref, bf16[4,4,256,256]{3,2,1,0:T(8,128)(2,1)} %get-tuple-element.45.q_ref, ...), custom_call_target="tpu_custom_call" | custom-call | tf_op jit(solution)/shard_map/pallas_call | solution.py:582
  79.3 26.3 %shard_map.205 = (f32[256,768]{1,0:T(8,128)}, f32[256,768]{1,0:T(8,128)}, f32[2,768]{1,0:T(2,128)}, bf16[4,256,192]{2,1,0:T(8,128)(2,1)}, f32[4,8,256]{2,1,0:T(8...) custom-call(s32[1]{0:T(128)S(6)} %add.10.length_ref, ...), custom_call_target="tpu_custom_call" | custom-call | tf_op jit(solution)/shard_map/pallas_call | solution.py:1509
  105.6 66.3 %shard_map.206 = (bf16[4,4,256,256]{3,2,1,0:T(8,128)(2,1)}, bf16[4,256,256]{2,1,0:T(8,128)(2,1)}, bf16[4,256,192]{2,1,0:T(8,128)(2,1)}, bf16[4,96,768]{2,1,0:T(8...) custom-call(bf16[4,4,256,256]{3,2,1,0:T(8,128)(2,1)} %get-tuple-element.45.q_ref, ...), custom_call_target="tpu_custom_call" | custom-call | tf_op jit(solution)/shard_map/pallas_call | solution.py:814
  171.9 107.7 %shard_map.207 = (bf16[8,96,2304]{2,1,0:T(8,128)(2,1)}, bf16[4,256,768]{2,1,0:T(8,128)(2,1)}, f32[8,768]{1,0:T(8,128)}, bf16[2,4,4,96,768]{4,3,2,1,0:T(8,128)(2,...) custom-call(bf16[4,4,256,256]{3,2,1,0:T(8,128)(2,1)} %get-tuple-element.58.query_ref, ...), custom_call_target="tpu_custom_call" | custom-call | tf_op jit(solution)/shard_map/pallas_call | solution.py:1227
  279.6 1.3 fusion
  282.2 1.5 slice_reduce_fusion
  283.7 0.0 copy-start
  283.7 16.6 %shard_map.208 = (f32[256,768]{1,0:T(8,128)}, f32[768,2304]{1,0:T(8,128)}, f32[768,768]{1,0:T(8,128)}, f32[768,3072]{1,0:T(8,128)}, f32[3072,768]{1,0:T(8,128)}) custom-call(f32[256,768]{1,0:T(8,128)} %bitcast.15, f32[768]{0:T(1024)} %gain_ref.7, f32[256,768]{1,0:T(8,128)} %get-tuple-element.51.resid_ref, bf16[4,256,768]{2,1,0:T(8,128)(2,1)} %get-tuple-element.68.home_ref, ...), custom_call_target="tpu_custom_call" | custom-call | tf_op jit(solution)/shard_map/pallas_call | solution.py:1584
  300.4 0.0 copy-done
  300.4 0.9 copy.26
Async XLA Ops:
  283.7 16.6 %copy-start = (f32[256,768]{1,0:T(8,128)S(1)}, f32[256,768]{1,0:T(8,128)}, u32[]{:S(2)}) copy-start(f32[256,768]{1,0:T(8,128)} %get-tuple-element.50) | copy-start | bytes 2359300

commit v2 on v1

--- a/solution.py
+++ b/solution.py
@@ -39,7 +39,7 @@
     return {"team": count // TEAMS, "lane": TEAMS, "core": 2, "all": count}[scope]
 
 
-def greet(scopes):
+def greet(scopes, meanwhile=None):
     barrier = pltpu.get_barrier_semaphore()
     number = 0
     for scope in scopes:
@@ -49,6 +49,8 @@
                 barrier, inc=1, device_id=device_of(lax.rem(mine + k, peers)), device_id_type=MESH
             )
         number += peers - 1
+    if meanwhile is not None:
+        meanwhile()
     pl.semaphore_wait(barrier, number)
 
 
@@ -202,15 +204,17 @@
         )
     for load in loads:
         load.start()
-    tokens = tokens_ref[...]
-    row_mean = jnp.mean(tokens, axis=1, keepdims=True)
-    centred = tokens - row_mean
-    variance = jnp.mean(centred * centred, axis=1, keepdims=True)
-    normed = (
-        centred * lax.rsqrt(variance + epsilon) * gain_ref[...][None, :] + bias_ref[...][None, :]
-    )
-    held[team] = normed.astype(jnp.bfloat16)
-    greet(["team", "lane"])
+    def norm():
+        tokens = tokens_ref[...]
+        row_mean = jnp.mean(tokens, axis=1, keepdims=True)
+        centred = tokens - row_mean
+        variance = jnp.mean(centred * centred, axis=1, keepdims=True)
+        normed = (
+            centred * lax.rsqrt(variance + epsilon) * gain_ref[...][None, :] + bias_ref[...][None, :]
+        )
+        held[team] = normed.astype(jnp.bfloat16)
+
+    greet(["team", "lane"], norm)
 
     def hop(side, distance, start=True):
         block = team - distance if side == 0 else team + distance
@@ -753,20 +757,19 @@
         every = jnp.full((rows, rows), -scale, jnp.bfloat16)
         last = ((count - 1) * lanes + lane) * rows + key_iota
         query_pos = i * rows + query_iota
-        sums = [None] * (TEAM_HEADS + 1)
-        for z in range(count):
-            carried = carried_ref[0, z]
-            total = None
-            for h in range(TEAM_HEADS):
-                probs = jnp.exp(dot(key_heads[h, z], q_row[h]) - carried - mass[h])
+        lows = [[] for _ in range(TEAM_HEADS + 1)]
+        totals = [None] * count
+        for h in range(TEAM_HEADS):
+            for z in range(count):
+                probs = jnp.exp(dot(key_heads[h, z], q_row[h]) - carried_ref[0, z] - mass[h])
                 value_sum[h, z] += dot(probs.astype(jnp.bfloat16), grad_col[h])
                 grad_logit = probs * (dot(value_heads[h, z], grad_row[h]) - inner[h])
-                total = grad_logit if h == 0 else total + grad_logit
+                totals[z] = grad_logit if h == 0 else totals[z] + grad_logit
                 low = grad_logit.astype(jnp.bfloat16)
                 key_sum[h, z] += dot(low, q_col[h])
-                part = dot(key_rows[z, span[h], :], low)
-                sums[h] = part if z == 0 else sums[h] + part
-            total = total.astype(jnp.bfloat16)
+                lows[h].append(low)
+        for z in range(count):
+            total = totals[z].astype(jnp.bfloat16)
             select_grad = running[z] + dot(total, later)
             running[z] = running[z] + dot(total, every)
             first = dot(key_heads[TEAM_HEADS, z], q_row[TEAM_HEADS])
@@ -775,10 +778,11 @@
                 live = live & (last < query_pos)
             low = jnp.where(live, select_grad, 0.0).astype(jnp.bfloat16)
             key_sum[TEAM_HEADS, z] += dot(low, q_col[TEAM_HEADS])
-            part = dot(key_rows[z, span[TEAM_HEADS], :], low)
-            sums[TEAM_HEADS] = part if z == 0 else sums[TEAM_HEADS] + part
+            lows[TEAM_HEADS].append(low)
         for h in range(TEAM_HEADS + 1):
-            query_grad_ref[0, 0, span[h], :] = sums[h].astype(jnp.bfloat16)
+            left = jnp.concatenate([key_rows[z, span[h], :] for z in range(count)], axis=1)
+            result = dot(left, jnp.concatenate(lows[h], axis=0))
+            query_grad_ref[0, 0, span[h], :] = result.astype(jnp.bfloat16)
 
     for count in range(1, TEAMS + 1):
         pl.when(active == count)(functools.partial(work, count))
@@ -927,46 +931,31 @@
         return other, {"seq": other * lanes + lane}
 
     sibling = {"batch": 1 - core}
-    greet(["core", "team", "lane"])
+    spans = (slice(0, QUERY_WIDTH), slice(QUERY_WIDTH, 2 * QUERY_WIDTH), slice(2 * QUERY_WIDTH, None))
+
+    def turn():
+        for span in spans:
+            weight_rows[span, :] = weight_ref[:, span].T
+        weight_grad[...] = jnp.zeros_like(weight_grad)
+
+    greet(["core", "team", "lane"], turn)
     first_sources = (query_ref, down_in, up_in, out_in)
     first_targets = (query_parts, down_parts, up_parts, out_parts)
     first_plan = [("team", "spread"), ("team", "spread"), ("lane", "spread"), ("lane", "spread")]
-    first_copies = [[], []]
+    first_copies = [[], [], []]
     for n in (1, 2, 3, 0):
         mine = peers_of(first_plan[n][0])[0]
         own = pltpu.make_async_copy(first_sources[n].at[mine], first_targets[n].at[mine], first_local.at[n])
         own.start()
-        first_copies[n == 0].append(own)
-        first_copies[n == 0] += remote_copies(
+        group = (2, 0, 1, 1)[n]
+        first_copies[group].append(own)
+        first_copies[group] += remote_copies(
             first_plan[n : n + 1],
             first_sources[n : n + 1],
             first_targets[n : n + 1],
             first_send.at[n : n + 1],
             first_recv.at[n : n + 1],
         )
-    spans = (slice(0, QUERY_WIDTH), slice(QUERY_WIDTH, 2 * QUERY_WIDTH), slice(2 * QUERY_WIDTH, None))
-    for span in spans:
-        weight_rows[span, :] = weight_ref[:, span].T
-    weight_grad[...] = jnp.zeros_like(weight_grad)
-
-    def known(b, _):
-        rows_low = lane_ref[b].T
-        turned[b] = rows_low
-        total = None
-        for span, grads in ((spans[1], key_ref[b]), (spans[2], value_ref[b])):
-            weight_grad[:, span] += dot(rows_low, grads)
-            part = dot(grads, weight_rows[span, :])
-            total = part if total is None else total + part
-        rows_sum[b] = total
-        return 0
-
-    lax.fori_loop(0, TEAMS, known, 0)
-    for copy in first_copies[0]:
-        copy.wait()
-    down_ref[...] = added([down_parts[k] for k in range(lanes)])
-    up_ref[...] = added([up_parts[k] for k in range(TEAMS)])
-    out_ref[...] = added([out_parts[k] for k in range(TEAMS)])
-
     def place(n, p, t, part=None):
         if n == 0:
             ref, start, wide = whole_down.at[core, p, t], 0, whole_down.shape[4]
@@ -998,27 +987,23 @@
     early = (down_ref, up_ref, out_ref)
     number = len(early)
     early_z = [[None] * TEAMS for _ in range(number)]
-    for k in range(1, TEAMS):
-        _, target = team_peer(k)
-        for n in range(number):
-            early_z[n][k] = push(
-                early[n],
-                place(n, lane, team),
-                early_team.at[0, n, k],
-                early_team.at[1, n, k],
-                target,
-            )
     early_kept = []
-    for n in range(number):
+
+    def publish(n):
+        for k in range(1, TEAMS):
+            _, target = team_peer(k)
+            sems = [early_team.at[side, n, k] for side in range(2)]
+            early_z[n][k] = push(early[n], place(n, lane, team), *sems, target)
         copy = pltpu.make_async_copy(early[n], place(n, lane, team), early_local.at[n])
         copy.start()
         early_kept.append(copy)
+
     early_out = []
     early_sib = []
 
-    def forward(j):
+    def forward(j, chosen=(0, 1, 2)):
         t = lax.rem(team - j + TEAMS, TEAMS)
-        for n in range(number):
+        for n in chosen:
             if j == 0:
                 source = early[n]
             else:
@@ -1055,8 +1040,32 @@
             sems = [early_core.at[side, n, j, 3] for side in range(2)]
             early_sib.append(push(piece, piece, *sems, sibling))
 
-    forward(0)
+    for copy in first_copies[0]:
+        copy.wait()
+    down_ref[...] = added([down_parts[k] for k in range(lanes)])
+    publish(0)
+    forward(0, (0,))
+
+    def known(b, _):
+        rows_low = lane_ref[b].T
+        turned[b] = rows_low
+        total = None
+        for span, grads in ((spans[1], key_ref[b]), (spans[2], value_ref[b])):
+            weight_grad[:, span] += dot(rows_low, grads)
+            part = dot(grads, weight_rows[span, :])
+            total = part if total is None else total + part
+        rows_sum[b] = total
+        return 0
+
+    lax.fori_loop(0, TEAMS, known, 0)
     for copy in first_copies[1]:
+        copy.wait()
+    up_ref[...] = added([up_parts[k] for k in range(TEAMS)])
+    out_ref[...] = added([out_parts[k] for k in range(TEAMS)])
+    publish(1)
+    publish(2)
+    forward(0, (1, 2))
+    for copy in first_copies[2]:
         copy.wait()
     gain = gain_ref[...][None, :]
     bias = bias_ref[...][None, :]
@@ -1555,10 +1564,21 @@
     )(length, mixed, masses, tokens, grad, gain, bias, w_out, w_up, w_down)
 
 
-def close_body(tokens_ref, gain_ref, resid_ref, home_ref, *refs):
-    grad_ref, rest = refs[len(refs) // 2], refs[: len(refs) // 2] + refs[len(refs) // 2 + 1 :]
-    for n in range(len(rest) // 2):
-        rest[len(rest) // 2 + n][...] = rest[n][...].astype(jnp.float32)
+def close_body(
+    tokens_ref,
+    gain_ref,
+    resid_ref,
+    home_ref,
+    layer_ref,
+    vector_ref,
+    *refs,
+):
+    count = (len(refs) - 6) // 2
+    weights, refs = refs[:count], refs[count:]
+    grad_ref, layer_out, *refs = refs
+    for source, target in zip(weights, refs[:count]):
+        target[...] = source[...].astype(jnp.float32)
+    layer_out[...] = layer_ref[...]
     tokens = tokens_ref[...]
     centred = tokens - jnp.mean(tokens, axis=1, keepdims=True)
     spread = lax.rsqrt(jnp.mean(centred * centred, axis=1, keepdims=True) + epsilon)
@@ -1573,28 +1593,38 @@
         - scaled * jnp.mean(inner * scaled, axis=1, keepdims=True)
     )
 
-
-def close(tokens, gain, resid, home, weights):
-    steps = 8
+    @pl.when(pl.program_id(0) == 0)
+    def _():
+        for n in range(4):
+            refs[count + n][...] = vector_ref[n]
+
+
+def close(tokens, gain, resid, home, layer, vectors, weights):
+    steps = 4
     rows, width = tokens.shape
 
     def band(x):
         return pl.BlockSpec((x.shape[0] // steps, x.shape[1]), lambda i: (i, 0))
 
+    line = pl.BlockSpec((width,), lambda i: (0,))
+    large = [tokens, layer] + weights
     return pl.pallas_call(
         close_body,
         grid=(steps,),
         in_specs=[
             band(tokens),
-            pl.BlockSpec((width,), lambda i: (0,)),
+            line,
             band(resid),
             pl.BlockSpec((TEAMS, rows // steps, width), lambda i: (0, i, 0)),
+            band(layer),
+            pl.BlockSpec(vectors.shape, lambda i: (0, 0)),
         ]
         + [band(x) for x in weights],
-        out_specs=[band(tokens)] + [band(x) for x in weights],
-        out_shape=[jax.ShapeDtypeStruct(x.shape, jnp.float32) for x in [tokens] + weights],
+        out_specs=[band(x) for x in large] + [line] * 4,
+        out_shape=[jax.ShapeDtypeStruct(x.shape, jnp.float32) for x in large]
+        + [jax.ShapeDtypeStruct((width,), jnp.float32)] * 4,
         compiler_params=pltpu.CompilerParams(vmem_limit_bytes=VMEM_BYTES),
-    )(tokens, gain, resid, home, *weights)
+    )(tokens, gain, resid, home, layer, vectors, *weights)
 
 
 def per_device(
@@ -1660,11 +1690,14 @@
         halves,
         6,
     )
-    grad_x, grad_w_qkv, grad_w_out, grad_w_up, grad_w_down = close(
+    pruned_share = (vectors[4, 0] / vectors[5, 0]).reshape(1)
+    grad_x, layer_out, grad_w_qkv, grad_w_out, grad_w_up, grad_w_down, *lines = close(
         tokens,
         ln1_gain,
         grad_resid,
         home_rows,
+        layer_out,
+        vectors,
         [
             grad_w_qkv.reshape(w_qkv.shape),
             grad_w_out.reshape(w_out.shape),
@@ -1672,16 +1705,15 @@
             grad_w_down.reshape(w_down.shape),
         ],
     )
-    pruned_share = (vectors[4, 0] / vectors[5, 0]).reshape(1)
     return (
         layer_out[None],
         grad_x[None],
-        vectors[0],
-        vectors[1],
+        lines[0],
+        lines[1],
         grad_w_qkv,
         grad_w_out,
-        vectors[2],
-        vectors[3],
+        lines[2],
+        lines[3],
         grad_w_up,
         grad_w_down,
         pruned_share,

time: 306 us -> 303 us (level)
  no operation moved by 1% of the time
where the time goes in v2:
time: 303 us; the launch traced here: 300 us
  Pallas kernels  294 us (97%)
  between operations  4.5 us (1%)
    pallas_call x1, Pallas kernels, finish(): pl.pallas_call(finish_body, out_shape=[jax.ShapeDtypeStruct((chunks, dept...  108 us
    pallas_call x1, Pallas kernels, attend_back(): pl.pallas_call(functools.partial(attend_back_body, blocks=blocks, rows=ro...  66.2 us
    pallas_call x1, Pallas kernels, project(): pl.pallas_call(project_body, out_shape=[jax.ShapeDtypeStruct((TEAMS, rows...  42.6 us
    pallas_call x1, Pallas kernels, attend(): pl.pallas_call(functools.partial(attend_body, blocks=blocks, rows=rows),...  34.4 us
    pallas_call x1, Pallas kernels, dense(): pl.pallas_call(dense_body, out_shape=[jax.ShapeDtypeStruct((rows, width),...  26.4 us
    pallas_call x1, Pallas kernels, close(): pl.pallas_call(close_body, grid=(steps,), in_specs=[band(tokens), line, b...  17.1 us

profile of v2, /device:TPU:0, one launch (start us, length us, event | category | flops | bytes accessed | tf_op | source)
XLA Modules:
  0.0 300.3 jit_solution(7916472317153796124)
XLA Ops:
  2.0 42.6 %shard_map.203 = (bf16[4,256,768]{2,1,0:T(8,128)(2,1)}, bf16[768,704]{1,0:T(8,128)(2,1)}, bf16[4,4,256,256]{3,2,1,0:T(8,128)(2,1)}, bf16[4,256,256]{2,1,0:T(8,128)(2,1)}, bf16[4,256,192]{2,1,0:T(8,128)(2,1)}) custom-call(f32[256,768]{1,0:T(8,128)} %bitcast.13, f32[768]{0:T(1024)} %gain_ref.7, f32[768]{0:T(1024)} %bias_ref.5, bf16[768,2304]{1,0:T(8,128)(2,1)} %w_ref.1), custom_call_target="tpu_custom_call" | custom-call | tf_op jit(solution)/shard_map/pallas_call | solution.py:327
  44.5 34.4 %shard_map.204 = (bf16[4,192,256]{2,1,0:T(8,128)(2,1)}, f32[4,8,256]{2,1,0:T(8,128)}, f32[16,4,256,256]{3,2,1,0:T(8,128)}, f32[8,256]{1,0:T(8,128)}) custom-call(s32[1]{0:T(128)S(6)} %add.10.length_ref, f32[1]{0:T(128)S(6)} %div.7.threshold_ref, bf16[4,4,256,256]{3,2,1,0:T(8,128)(2,1)} %get-tuple-element.50.q_ref, ...), custom_call_target="tpu_custom_call" | custom-call | tf_op jit(solution)/shard_map/pallas_call | solution.py:586
  78.9 26.4 %shard_map.205 = (f32[256,768]{1,0:T(8,128)}, f32[256,768]{1,0:T(8,128)}, f32[2,768]{1,0:T(2,128)}, bf16[4,256,192]{2,1,0:T(8,128)(2,1)}, f32[4,8,256]{2,1,0:T(8...) custom-call(s32[1]{0:T(128)S(6)} %add.10.length_ref, ...), custom_call_target="tpu_custom_call" | custom-call | tf_op jit(solution)/shard_map/pallas_call | solution.py:1518
  105.3 66.2 %shard_map.206 = (bf16[4,4,256,256]{3,2,1,0:T(8,128)(2,1)}, bf16[4,256,256]{2,1,0:T(8,128)(2,1)}, bf16[4,256,192]{2,1,0:T(8,128)(2,1)}, bf16[4,96,768]{2,1,0:T(8...) custom-call(bf16[4,4,256,256]{3,2,1,0:T(8,128)(2,1)} %get-tuple-element.50.q_ref, ...), custom_call_target="tpu_custom_call" | custom-call | tf_op jit(solution)/shard_map/pallas_call | solution.py:818
  171.5 107.9 %shard_map.207 = (bf16[8,96,2304]{2,1,0:T(8,128)(2,1)}, bf16[4,256,768]{2,1,0:T(8,128)(2,1)}, f32[8,768]{1,0:T(8,128)}, bf16[2,4,4,96,768]{4,3,2,1,0:T(8,128)(2,...) custom-call(bf16[4,4,256,256]{3,2,1,0:T(8,128)(2,1)} %get-tuple-element.62.query_ref, ...), custom_call_target="tpu_custom_call" | custom-call | tf_op jit(solution)/shard_map/pallas_call | solution.py:1236
  279.4 17.1 %shard_map.208 = (f32[256,768]{1,0:T(8,128)}, f32[256,768]{1,0:T(8,128)}, f32[768,2304]{1,0:T(8,128)}, f32[768,768]{1,0:T(8,128)}, f32[768,3072]{1,0:T(8,128)}, ...) custom-call(f32[256,768]{1,0:T(8,128)} %bitcast.15, f32[768]{0:T(1024)} %gain_ref.7, ...), custom_call_target="tpu_custom_call" | custom-call | tf_op jit(solution)/shard_map/pallas_call | solution.py:1611
  296.5 1.3 fusion

commit v3 on v2

--- a/solution.py
+++ b/solution.py
@@ -1105,7 +1105,6 @@
     ]
     for copy in core_copies:
         copy.wait()
-    relay(0)
 
     both = vector_ref[...] + vectors[0]
     vectors[1 + lane] = both
@@ -1145,6 +1144,7 @@
             push(team_send_main, team_main.at[team], team_sems.at[0, 0, k], team_sems.at[1, 0, k], target),
             push(ready.at[1], vectors.at[1 + lanes + team], vector_sems.at[0, at], vector_sems.at[1, at], target),
         ]
+    relay(0)
     home_copies = []
     for k in range(1, TEAMS):
         other, target = team_peer(k)

time: 303 us -> 301 us (level)
  no operation moved by 1% of the time
where the time goes in v3:
time: 301 us
  Pallas kernels  295 us (98%)
  between operations  4.5 us (1%)
    pallas_call x1, Pallas kernels, finish(): pl.pallas_call(finish_body, out_shape=[jax.ShapeDtypeStruct((chunks, dept...  108 us
    pallas_call x1, Pallas kernels, attend_back(): pl.pallas_call(functools.partial(attend_back_body, blocks=blocks, rows=ro...  66.2 us
    pallas_call x1, Pallas kernels, project(): pl.pallas_call(project_body, out_shape=[jax.ShapeDtypeStruct((TEAMS, rows...  42.6 us
    pallas_call x1, Pallas kernels, attend(): pl.pallas_call(functools.partial(attend_body, blocks=blocks, rows=rows),...  34.4 us
    pallas_call x1, Pallas kernels, dense(): pl.pallas_call(dense_body, out_shape=[jax.ShapeDtypeStruct((rows, width),...  26.4 us
    pallas_call x1, Pallas kernels, close(): pl.pallas_call(close_body, grid=(steps,), in_specs=[band(tokens), line, b...  17.1 us

profile of v3, /device:TPU:0, one launch (start us, length us, event | category | flops | bytes accessed | tf_op | source)
XLA Modules:
  0.0 300.5 jit_solution(7657945818087707588)
XLA Ops:
  2.0 42.6 %shard_map.203 = (bf16[4,256,768]{2,1,0:T(8,128)(2,1)}, bf16[768,704]{1,0:T(8,128)(2,1)}, bf16[4,4,256,256]{3,2,1,0:T(8,128)(2,1)}, bf16[4,256,256]{2,1,0:T(8,128)(2,1)}, bf16[4,256,192]{2,1,0:T(8,128)(2,1)}) custom-call(f32[256,768]{1,0:T(8,128)} %bitcast.13, f32[768]{0:T(1024)} %gain_ref.7, f32[768]{0:T(1024)} %bias_ref.5, bf16[768,2304]{1,0:T(8,128)(2,1)} %w_ref.1), custom_call_target="tpu_custom_call" | custom-call | tf_op jit(solution)/shard_map/pallas_call | solution.py:327
  44.5 34.4 %shard_map.204 = (bf16[4,192,256]{2,1,0:T(8,128)(2,1)}, f32[4,8,256]{2,1,0:T(8,128)}, f32[16,4,256,256]{3,2,1,0:T(8,128)}, f32[8,256]{1,0:T(8,128)}) custom-call(s32[1]{0:T(128)S(6)} %add.10.length_ref, f32[1]{0:T(128)S(6)} %div.7.threshold_ref, bf16[4,4,256,256]{3,2,1,0:T(8,128)(2,1)} %get-tuple-element.50.q_ref, ...), custom_call_target="tpu_custom_call" | custom-call | tf_op jit(solution)/shard_map/pallas_call | solution.py:586
  78.9 26.4 %shard_map.205 = (f32[256,768]{1,0:T(8,128)}, f32[256,768]{1,0:T(8,128)}, f32[2,768]{1,0:T(2,128)}, bf16[4,256,192]{2,1,0:T(8,128)(2,1)}, f32[4,8,256]{2,1,0:T(8...) custom-call(s32[1]{0:T(128)S(6)} %add.10.length_ref, ...), custom_call_target="tpu_custom_call" | custom-call | tf_op jit(solution)/shard_map/pallas_call | solution.py:1518
  105.3 66.2 %shard_map.206 = (bf16[4,4,256,256]{3,2,1,0:T(8,128)(2,1)}, bf16[4,256,256]{2,1,0:T(8,128)(2,1)}, bf16[4,256,192]{2,1,0:T(8,128)(2,1)}, bf16[4,96,768]{2,1,0:T(8...) custom-call(bf16[4,4,256,256]{3,2,1,0:T(8,128)(2,1)} %get-tuple-element.50.q_ref, ...), custom_call_target="tpu_custom_call" | custom-call | tf_op jit(solution)/shard_map/pallas_call | solution.py:818
  171.5 108.1 %shard_map.207 = (bf16[8,96,2304]{2,1,0:T(8,128)(2,1)}, bf16[4,256,768]{2,1,0:T(8,128)(2,1)}, f32[8,768]{1,0:T(8,128)}, bf16[2,4,4,96,768]{4,3,2,1,0:T(8,128)(2,...) custom-call(bf16[4,4,256,256]{3,2,1,0:T(8,128)(2,1)} %get-tuple-element.62.query_ref, ...), custom_call_target="tpu_custom_call" | custom-call | tf_op jit(solution)/shard_map/pallas_call | solution.py:1236
  279.6 17.1 %shard_map.208 = (f32[256,768]{1,0:T(8,128)}, f32[256,768]{1,0:T(8,128)}, f32[768,2304]{1,0:T(8,128)}, f32[768,768]{1,0:T(8,128)}, f32[768,3072]{1,0:T(8,128)}, ...) custom-call(f32[256,768]{1,0:T(8,128)} %bitcast.15, f32[768]{0:T(1024)} %gain_ref.7, ...), custom_call_target="tpu_custom_call" | custom-call | tf_op jit(solution)/shard_map/pallas_call | solution.py:1611
  296.7 1.3 fusion

commit v4 on v3

--- a/solution.py
+++ b/solution.py
@@ -1359,7 +1359,6 @@
     ]
     for load in loads:
         load.start()
-    greet(["core", "lane"])
 
     def half_of(ref, which):
         half = ref.shape[1] // 2
@@ -1386,14 +1385,19 @@
         )
 
     grad_top = grad_ref[...]
-    top[...] = grad_top.astype(jnp.bfloat16)
-    swap(1, True)
     valid = me * rows + lax.broadcasted_iota(jnp.int32, (rows, width), 0) < length_ref[0]
     mixed_rows = mixed_ref[...]
-    mixed[...] = jnp.where(valid, mixed_rows.T, jnp.zeros((), jnp.bfloat16))
+
+    def prepare():
+        top[...] = grad_top.astype(jnp.bfloat16)
+        mixed[...] = jnp.where(valid, mixed_rows.T, jnp.zeros((), jnp.bfloat16))
+        loads[0].wait()
+        total[...] = tokens_ref[...] + dot(mixed[...], w_out[...])
+
+    greet(["core", "lane"], prepare)
+    swap(1, True)
     swap(4, True)
-    loads[0].wait()
-    residual = tokens_ref[...] + dot(mixed[...], w_out[...])
+    residual = total[...]
     row_mean = jnp.mean(residual, axis=1, keepdims=True)
     centred = residual - row_mean
     variance = jnp.mean(centred * centred, axis=1, keepdims=True)
@@ -1402,7 +1406,6 @@
     gain = gain_ref[...][None, :]
     normed[...] = (scaled * gain + bias_ref[...][None, :]).astype(jnp.bfloat16)
     swap(2, True)
-    total[...] = residual
     back[...] = jnp.zeros_like(back)
     loads[1].wait()
     loads[2].wait()

time: 301 us -> 301 us (level)
  no operation moved by 1% of the time
where the time goes in v4:
time: 301 us
  Pallas kernels  295 us (98%)
  between operations  4.5 us (1%)
    pallas_call x1, Pallas kernels, finish(): pl.pallas_call(finish_body, out_shape=[jax.ShapeDtypeStruct((chunks, dept...  108 us
    pallas_call x1, Pallas kernels, attend_back(): pl.pallas_call(functools.partial(attend_back_body, blocks=blocks, rows=ro...  66.4 us
    pallas_call x1, Pallas kernels, project(): pl.pallas_call(project_body, out_shape=[jax.ShapeDtypeStruct((TEAMS, rows...  42.6 us
    pallas_call x1, Pallas kernels, attend(): pl.pallas_call(functools.partial(attend_body, blocks=blocks, rows=rows),...  34.4 us
    pallas_call x1, Pallas kernels, dense(): pl.pallas_call(dense_body, out_shape=[jax.ShapeDtypeStruct((rows, width),...  25.7 us
    pallas_call x1, Pallas kernels, close(): pl.pallas_call(close_body, grid=(steps,), in_specs=[band(tokens), line, b...  17.1 us

profile of v4, /device:TPU:0, one launch (start us, length us, event | category | flops | bytes accessed | tf_op | source)
XLA Modules:
  0.0 300.5 jit_solution(1914494871929322645)
XLA Ops:
  2.0 42.6 %shard_map.203 = (bf16[4,256,768]{2,1,0:T(8,128)(2,1)}, bf16[768,704]{1,0:T(8,128)(2,1)}, bf16[4,4,256,256]{3,2,1,0:T(8,128)(2,1)}, bf16[4,256,256]{2,1,0:T(8,128)(2,1)}, bf16[4,256,192]{2,1,0:T(8,128)(2,1)}) custom-call(f32[256,768]{1,0:T(8,128)} %bitcast.13, f32[768]{0:T(1024)} %gain_ref.7, f32[768]{0:T(1024)} %bias_ref.5, bf16[768,2304]{1,0:T(8,128)(2,1)} %w_ref.1), custom_call_target="tpu_custom_call" | custom-call | tf_op jit(solution)/shard_map/pallas_call | solution.py:327
  44.5 34.4 %shard_map.204 = (bf16[4,192,256]{2,1,0:T(8,128)(2,1)}, f32[4,8,256]{2,1,0:T(8,128)}, f32[16,4,256,256]{3,2,1,0:T(8,128)}, f32[8,256]{1,0:T(8,128)}) custom-call(s32[1]{0:T(128)S(6)} %add.10.length_ref, f32[1]{0:T(128)S(6)} %div.7.threshold_ref, bf16[4,4,256,256]{3,2,1,0:T(8,128)(2,1)} %get-tuple-element.50.q_ref, ...), custom_call_target="tpu_custom_call" | custom-call | tf_op jit(solution)/shard_map/pallas_call | solution.py:586
  78.9 25.7 %shard_map.205 = (f32[256,768]{1,0:T(8,128)}, f32[256,768]{1,0:T(8,128)}, f32[2,768]{1,0:T(2,128)}, bf16[4,256,192]{2,1,0:T(8,128)(2,1)}, f32[4,8,256]{2,1,0:T(8...) custom-call(s32[1]{0:T(128)S(6)} %add.10.length_ref, ...), custom_call_target="tpu_custom_call" | custom-call | tf_op jit(solution)/shard_map/pallas_call | solution.py:1521
  104.7 66.4 %shard_map.206 = (bf16[4,4,256,256]{3,2,1,0:T(8,128)(2,1)}, bf16[4,256,256]{2,1,0:T(8,128)(2,1)}, bf16[4,256,192]{2,1,0:T(8,128)(2,1)}, bf16[4,96,768]{2,1,0:T(8...) custom-call(bf16[4,4,256,256]{3,2,1,0:T(8,128)(2,1)} %get-tuple-element.50.q_ref, ...), custom_call_target="tpu_custom_call" | custom-call | tf_op jit(solution)/shard_map/pallas_call | solution.py:818
  171.2 108.4 %shard_map.207 = (bf16[8,96,2304]{2,1,0:T(8,128)(2,1)}, bf16[4,256,768]{2,1,0:T(8,128)(2,1)}, f32[8,768]{1,0:T(8,128)}, bf16[2,4,4,96,768]{4,3,2,1,0:T(8,128)(2,...) custom-call(bf16[4,4,256,256]{3,2,1,0:T(8,128)(2,1)} %get-tuple-element.62.query_ref, ...), custom_call_target="tpu_custom_call" | custom-call | tf_op jit(solution)/shard_map/pallas_call | solution.py:1236
  279.6 17.1 %shard_map.208 = (f32[256,768]{1,0:T(8,128)}, f32[256,768]{1,0:T(8,128)}, f32[768,2304]{1,0:T(8,128)}, f32[768,768]{1,0:T(8,128)}, f32[768,3072]{1,0:T(8,128)}, ...) custom-call(f32[256,768]{1,0:T(8,128)} %bitcast.15, f32[768]{0:T(1024)} %gain_ref.7, ...), custom_call_target="tpu_custom_call" | custom-call | tf_op jit(solution)/shard_map/pallas_call | solution.py:1614
  296.7 1.3 fusion
